TPU v7x, 128 devices: a whole 4x4x4 slice. The times are simulated.
128 devices in a mesh: ep: 64 (over z, y, x), hd: 2 (over core).
Axes of the slice: x: 4, y: 4, z: 4, core: 2. Of those that a mesh axis runs over, the one named last changes fastest.
Arguments:
- hidden_in: bfloat16 [512, 3, 2048], P('ep'), may hold values from -6 to 6
- new_queries: bfloat16 [512, 3, 16, 128], P('ep', None, 'hd'), may hold values from -6 to 6
- new_keys: bfloat16 [512, 3, 16, 128], P('ep', None, 'hd'), may hold values from -6 to 6
- new_values: bfloat16 [512, 3, 32, 128], P('ep', None, 'hd'), may hold values from -6 to 6
- out_gate: bfloat16 [512, 3, 32, 128], P('ep', None, 'hd'), may hold values from -6 to 6
- decay_logit: bfloat16 [512, 3, 32], P('ep', None, 'hd'), may hold values from -6 to 6
- write_logit: bfloat16 [512, 3, 32], P('ep', None, 'hd'), may hold values from -6 to 6
- decay_scale: float32 [32], P('hd'), may hold values from -2 to 1.5
- decay_bias: float32 [32], P('hd'), may hold values from -2 to 1
- head_gain: float32 [128], replicated, may hold values from 0.1 to 1.9
- out_projection: bfloat16 [4096, 2048], P('hd'), may hold values from -0.09375 to 0.09375
- norm_gain: float32 [2048], replicated, may hold values from 0.1 to 1.9
- expert_ids: int32 [512, 3, 10], P('ep'), may hold values from 0 to 127, all different within a row; in each aligned block of 24 rows (0 to 23, 24 to 47, ..., all dimensions but the last counted through in order) at most 3 rows name the same one
- route_weight: float32 [512, 3, 10], P('ep'), may hold values from 0.02 to 1
- gate_weight: bfloat16 [128, 2048, 512], P(('ep', 'hd')), may hold values from -0.125 to 0.125
- up_weight: bfloat16 [128, 2048, 512], P(('ep', 'hd')), may hold values from -0.125 to 0.125
- down_weight: bfloat16 [128, 512, 2048], P(('ep', 'hd')), may hold values from -0.25 to 0.25
- old_state: float32 [512, 32, 128, 128], P('ep', 'hd'), may hold values from -4 to 4
Outputs:
- output_rows: bfloat16 [512, 3, 2048], P('ep', None, 'hd')
- new_state: float32 [512, 32, 128, 128], P('ep', 'hd')
Inputs may be any that keep to these rules, and one draw needn't show every extreme that they name: `expert_ids`: each token names 10 different experts. Within each block of 24 tokens (the rows of one index of ep), no expert is named by more than 3 tokens, a bound that some block reaches.
All inputs are finite; a program needn't handle non-finite values.
Results may differ from a plain program's by a relative error of at most 0.013.
Values may be sent and summed in bfloat16 or wider, within the bound.
No kernel may reach another device: no remote copies, remote signals or barrier semaphores. Data moves between devices by JAX's collectives and lax.ppermute only.
A program may use at most 128 MiB of HBM per device.

v0:
```python
import jax
import jax.numpy as jnp
from jax import lax
from jax.experimental import pallas as pl
from jax.experimental.pallas import tpu as pltpu
from jax.sharding import PartitionSpec as P

EPSILON = 1e-06
F32 = jnp.float32
BF16 = jnp.bfloat16

R = 8
T = 3
TOK = R * T
HK = 8
D = 2048
FF = 512
SLOTS = 3
CHIPS = 64
PARTS = 8
PC = D // PARTS
TP = 32
MiB = 1 << 20


def dot(a, b, dims=((1,), (0,))):
    return lax.dot_general(a, b, (dims, ((), ())), preferred_element_type=F32)


def iota(shape, dim):
    return lax.broadcasted_iota(jnp.int32, shape, dim)


def core_kernel(
    q_ref, k_ref, v_ref, g_ref, a_ref, b_ref, scale_ref, bias_ref, gain_ref, h_ref, s_ref, w_ref,
    own_ref, send_ref, ku_ref, uu_ref, f3_ref,
    qs, ks, vs, gs, fs, bs, acc,
):
    hk = pl.program_id(0)

    @pl.when(hk == 0)
    def _():
        for t in range(T):
            for r in range(R):
                at = t * R + r
                qs[pl.ds(at, HK, stride=TOK), :] = q_ref[r, t].astype(F32)
                ks[pl.ds(at, HK, stride=TOK), :] = k_ref[r, t].astype(F32)
                v = v_ref[r, t].astype(F32)
                g = g_ref[r, t].astype(F32)
                g = g * (1.0 / (1.0 + jnp.exp(-g)))
                for half in range(2):
                    rows = pl.ds(half * HK * TOK + at, HK, stride=TOK)
                    vs[rows, :] = v[half * HK : (half + 1) * HK]
                    gs[rows, :] = g[half * HK : (half + 1) * HK]
        rate = -jnp.exp(scale_ref[...])
        a_all = a_ref[...].astype(F32)
        b_all = b_ref[...].astype(F32)
        for t in range(T):
            x = a_all[:, t, :] + bias_ref[...]
            soft = jnp.maximum(x, 0.0) + jnp.log1p(jnp.exp(-jnp.abs(x)))
            factor = jnp.exp(rate * soft)
            strength = 1.0 / (1.0 + jnp.exp(-b_all[:, t, :]))
            for h in range(2 * HK):
                rows = slice(h * TOK + t * R, h * TOK + (t + 1) * R)
                fs[rows, :] = jnp.broadcast_to(factor[:, h : h + 1], (R, 128))
                bs[rows, :] = jnp.broadcast_to(strength[:, h : h + 1], (R, 128))

    rows = pl.ds(pl.multiple_of(hk * TOK, 8), TOK)
    q = qs[rows, :]
    k = ks[rows, :]
    q = q * lax.rsqrt(jnp.sum(q * q, axis=-1, keepdims=True) + EPSILON)
    k = k * lax.rsqrt(jnp.sum(k * k, axis=-1, keepdims=True) + EPSILON)
    ku_ref[0] = k
    kq = jnp.concatenate([k, q], axis=0)
    row_of = iota((2 * TOK, 128), 0) % R
    lhs = jnp.concatenate([jnp.where(row_of == r, kq, 0.0) for r in range(R)], axis=1).astype(BF16)

    kt = [k[t * R : (t + 1) * R] for t in range(T)]
    qt = [q[t * R : (t + 1) * R] for t in range(T)]

    def pair(x, y):
        return jnp.sum(x * y, axis=-1, keepdims=True)

    kk21, kk31, kk32 = pair(kt[1], kt[0]), pair(kt[2], kt[0]), pair(kt[2], kt[1])
    qk = [[pair(qt[t], kt[s]) for s in range(t + 1)] for t in range(T)]
    heads = []
    gain = gain_ref[...]
    for j in range(2):
        state = s_ref[:, j].reshape(R * 128, 128).astype(BF16)
        both = dot(lhs, state)
        recall = [both[t * R : (t + 1) * R] for t in range(T)]
        seen = [both[TOK + t * R : TOK + (t + 1) * R] for t in range(T)]
        base = pl.multiple_of((2 * hk + j) * TOK, 8)
        f = [fs[pl.ds(base + t * R, R), :] for t in range(T)]
        b = [bs[pl.ds(base + t * R, R), :] for t in range(T)]
        v = [vs[pl.ds(base + t * R, R), :] for t in range(T)]
        f01 = f[0] * f[1]
        f12 = f[1] * f[2]
        f012 = f01 * f[2]
        u0 = b[0] * (v[0] - f[0] * recall[0])
        u1 = b[1] * (v[1] - f01 * recall[1] - f[1] * kk21 * u0)
        u2 = b[2] * (v[2] - f012 * recall[2] - f12 * kk31 * u0 - f[2] * kk32 * u1)
        c0 = f[0] * seen[0] + qk[0][0] * u0
        c1 = f01 * seen[1] + f[1] * qk[1][0] * u0 + qk[1][1] * u1
        c2 = f012 * seen[2] + f12 * qk[2][0] * u0 + f[2] * qk[2][1] * u1 + qk[2][2] * u2
        lanes = slice(j * 128, (j + 1) * 128)
        uu_ref[0, :, lanes] = jnp.concatenate([f12 * u0, f[2] * u1, u2], axis=0)
        f3_ref[0, :, lanes] = f012
        c = jnp.concatenate([c0, c1, c2], axis=0)
        normed = c * lax.rsqrt(jnp.mean(c * c, axis=-1, keepdims=True) + EPSILON) * gain
        heads.append((normed * gs[pl.ds(base, TOK), :]).astype(BF16))
    part = dot(jnp.concatenate(heads, axis=1), w_ref[...])

    @pl.when(hk == 0)
    def _():
        acc[...] = part

    @pl.when(hk > 0)
    def _():
        acc[...] += part

    @pl.when(hk == HK - 1)
    def _():
        total = acc[...]
        send_ref[...] = total.astype(BF16)
        hidden = h_ref[...].astype(F32)
        for t in range(T):
            own_ref[t * R : (t + 1) * R, :] = total[t * R : (t + 1) * R] + hidden[:, t, :]


def core_call(q, k, v, g, a, b, scale, bias, gain, hidden, state, w):
    def whole(x):
        zeros = (0,) * x.ndim
        return pl.BlockSpec(x.shape, lambda i: zeros)

    small = (q, k, v, g, a, b, scale, bias, gain, hidden)
    return pl.pallas_call(
        core_kernel,
        grid=(HK,),
        in_specs=[whole(x) for x in small]
        + [
            pl.BlockSpec((R, 2, 128, 128), lambda i: (0, i, 0, 0)),
            pl.BlockSpec((256, D), lambda i: (i, 0)),
        ],
        out_specs=[
            pl.BlockSpec((TOK, D), lambda i: (0, 0)),
            pl.BlockSpec((TOK, D), lambda i: (0, 0)),
            pl.BlockSpec((1, TOK, 128), lambda i: (i, 0, 0)),
            pl.BlockSpec((1, TOK, 256), lambda i: (i, 0, 0)),
            pl.BlockSpec((1, R, 256), lambda i: (i, 0, 0)),
        ],
        out_shape=[
            jax.ShapeDtypeStruct((TOK, D), F32),
            jax.ShapeDtypeStruct((TOK, D), BF16),
            jax.ShapeDtypeStruct((HK, TOK, 128), F32),
            jax.ShapeDtypeStruct((HK, TOK, 256), F32),
            jax.ShapeDtypeStruct((HK, R, 256), F32),
        ],
        scratch_shapes=[
            pltpu.VMEM((HK * TOK, 128), F32),
            pltpu.VMEM((HK * TOK, 128), F32),
            pltpu.VMEM((2 * HK * TOK, 128), F32),
            pltpu.VMEM((2 * HK * TOK, 128), F32),
            pltpu.VMEM((2 * HK * TOK, 128), F32),
            pltpu.VMEM((2 * HK * TOK, 128), F32),
            pltpu.VMEM((TOK, D), F32),
        ],
        compiler_params=pltpu.CompilerParams(vmem_limit_bytes=24 * MiB),
        cost_estimate=pl.CostEstimate(flops=10**9, bytes_accessed=17 * MiB, transcendentals=10**5),
        name="core",
    )(*small, state, w)


def state_kernel(s_ref, k_ref, u_ref, f_ref, o_ref):
    def split(x):
        high = x.astype(BF16).astype(F32)
        return high, x - high

    k_high, k_low = split(k_ref[0])
    u_high, u_low = split(u_ref[0])
    keys = jnp.concatenate([k_high, k_low, k_high], axis=0).T
    updates = jnp.concatenate([u_high, u_high, u_low], axis=0).astype(BF16)
    row_of = iota(keys.shape, 1) % R
    for r in range(R):
        own = jnp.where(row_of == r, keys, 0.0).astype(BF16)
        added = dot(own, updates)
        for j in range(2):
            lanes = slice(j * 128, (j + 1) * 128)
            o_ref[r, j] = s_ref[r, j] * f_ref[0, r : r + 1, lanes] + added[:, lanes]


def state_call(state, keys, updates, factor):
    return pl.pallas_call(
        state_kernel,
        grid=(HK,),
        in_specs=[
            pl.BlockSpec((R, 2, 128, 128), lambda i: (0, i, 0, 0)),
            pl.BlockSpec((1, TOK, 128), lambda i: (i, 0, 0)),
            pl.BlockSpec((1, TOK, 256), lambda i: (i, 0, 0)),
            pl.BlockSpec((1, R, 256), lambda i: (i, 0, 0)),
        ],
        out_specs=pl.BlockSpec((R, 2, 128, 128), lambda i: (0, i, 0, 0)),
        out_shape=jax.ShapeDtypeStruct(state.shape, F32),
        compiler_params=pltpu.CompilerParams(vmem_limit_bytes=16 * MiB),
        cost_estimate=pl.CostEstimate(flops=10**9, bytes_accessed=17 * MiB, transcendentals=0),
        name="state",
    )(state, keys, updates, factor)


def table_kernel(ids_ref, route_ref, pick_ref, mix_ref):
    parity = lax.axis_index("hd")
    ids3 = ids_ref[...]
    route3 = route_ref[...]
    ids = jnp.concatenate([ids3[:, t, :] for t in range(T)], axis=0)
    route = jnp.concatenate([route3[:, t, :] for t in range(T)], axis=0)
    mixing = route / jnp.sum(route, axis=1, keepdims=True)
    expert = iota((TOK, CHIPS), 1) * 2 + parity
    named = jnp.zeros((TOK, CHIPS), F32)
    weight = jnp.zeros((TOK, CHIPS), F32)
    for c in range(ids.shape[1]):
        hit = ids[:, c : c + 1] == expert
        named = jnp.where(hit, 1.0, named)
        weight = jnp.where(hit, mixing[:, c : c + 1], weight)
    earlier = (iota((TOK, TOK), 0) > iota((TOK, TOK), 1)).astype(F32)
    rank = dot(earlier.astype(BF16), named.astype(BF16))
    rows = CHIPS * PARTS
    pad = jnp.zeros((TP - TOK, CHIPS), F32)
    spread = (iota((rows, CHIPS), 0) // PARTS == iota((rows, CHIPS), 1)).astype(F32).astype(BF16)
    across = (iota((CHIPS, rows), 1) // PARTS == iota((CHIPS, rows), 0)).astype(F32).astype(BF16)
    tile = (iota((TP, PARTS * TP), 1) % TP == iota((TP, PARTS * TP), 0)).astype(F32).astype(BF16)
    keep = iota((rows, PARTS * TP), 0) % PARTS == iota((rows, PARTS * TP), 1) // TP
    for s in range(SLOTS):
        here = jnp.where((named > 0.5) & (jnp.abs(rank - s) < 0.5), 1.0, 0.0)
        chosen = jnp.concatenate([here, pad], axis=0)
        tiled = dot(chosen.astype(BF16), tile, ((0,), (0,)))
        full = dot(spread, tiled.astype(BF16))
        pick_ref[s] = jnp.where(keep, full, 0.0).astype(BF16)
        share = jnp.concatenate([weight * here, pad], axis=0)
        high = share.astype(BF16).astype(F32)
        parts = jnp.concatenate([high, share - high], axis=0).astype(BF16)
        mix_ref[s] = dot(parts, across).astype(BF16)


def table_call(ids, route):
    return pl.pallas_call(
        table_kernel,
        out_shape=[
            jax.ShapeDtypeStruct((SLOTS, CHIPS * PARTS, PARTS * TP), BF16),
            jax.ShapeDtypeStruct((SLOTS, 2 * TP, CHIPS * PARTS), BF16),
        ],
        compiler_params=pltpu.CompilerParams(vmem_limit_bytes=16 * MiB),
        cost_estimate=pl.CostEstimate(flops=10**8, bytes_accessed=10**6, transcendentals=0),
        name="tables",
    )(ids, route)


def dispatch_kernel(own_ref, got_ref, gain_ref, pick_ref, res_ref, out_ref):
    residual = own_ref[...] + got_ref[...].astype(F32)
    res_ref[...] = residual
    scale = lax.rsqrt(jnp.mean(residual * residual, axis=1, keepdims=True) + EPSILON)
    normed = residual * scale * gain_ref[...]
    pad = jnp.zeros((TP - TOK, PC), F32)
    pieces = []
    for p in range(PARTS):
        pieces += [normed[:, p * PC : (p + 1) * PC], pad]
    stacked = jnp.concatenate(pieces, axis=0).astype(BF16)
    for s in range(SLOTS):
        out_ref[:, s * PC : (s + 1) * PC] = dot(pick_ref[s], stacked).astype(BF16)


def dispatch_call(own, got, gain, pick):
    return pl.pallas_call(
        dispatch_kernel,
        out_shape=[
            jax.ShapeDtypeStruct((TOK, D), F32),
            jax.ShapeDtypeStruct((CHIPS * PARTS, SLOTS * PC), BF16),
        ],
        compiler_params=pltpu.CompilerParams(vmem_limit_bytes=16 * MiB),
        cost_estimate=pl.CostEstimate(flops=2 * 10**8, bytes_accessed=2 * 10**6, transcendentals=0),
        name="dispatch",
    )(own, got, gain, pick)


def expert_kernel(x_ref, gate_ref, up_ref, down_ref, y_ref, wide):
    chunks = SLOTS * PC // 128
    for c in range(chunks):
        wide[c] = x_ref[:, c * 128 : (c + 1) * 128].astype(F32)
    gate = jnp.zeros((SLOTS * CHIPS, FF), F32)
    up = jnp.zeros((SLOTS * CHIPS, FF), F32)
    for p in range(PARTS):
        rows = [wide[c, pl.ds(p, CHIPS, stride=PARTS), :] for c in range(chunks)]
        x = jnp.concatenate(
            [jnp.concatenate(rows[0::2], axis=0), jnp.concatenate(rows[1::2], axis=0)], axis=1
        ).astype(BF16)
        gate += dot(x, gate_ref[0, p * PC : (p + 1) * PC, :])
        up += dot(x, up_ref[0, p * PC : (p + 1) * PC, :])
    activated = (gate * (1.0 / (1.0 + jnp.exp(-gate))) * up).astype(BF16)
    for p in range(PARTS):
        y = dot(activated, down_ref[0, :, p * PC : (p + 1) * PC])
        for c in range(chunks):
            at, side = c // 2 * CHIPS, c % 2 * 128
            wide[c, pl.ds(p, CHIPS, stride=PARTS), :] = y[at : at + CHIPS, side : side + 128]
    for c in range(chunks):
        y_ref[:, c * 128 : (c + 1) * 128] = wide[c].astype(BF16)


def expert_call(x, gate, up, down):
    return pl.pallas_call(
        expert_kernel,
        out_shape=jax.ShapeDtypeStruct(x.shape, BF16),
        scratch_shapes=[pltpu.VMEM((x.shape[1] // 128, x.shape[0], 128), F32)],
        compiler_params=pltpu.CompilerParams(vmem_limit_bytes=24 * MiB),
        cost_estimate=pl.CostEstimate(flops=12 * 10**8, bytes_accessed=8 * 10**6, transcendentals=10**5),
        name="expert",
    )(x, gate, up, down)


def combine_kernel(y_ref, mix_ref, res_ref, keep_ref, send_ref):
    parity = lax.axis_index("hd")
    part_of = iota((2 * TP, CHIPS * PARTS), 1) % PARTS
    half = D // 2
    total = None
    for s in range(SLOTS):
        mix = mix_ref[s].astype(F32)
        rows = [jnp.where(part_of == p, mix, 0.0) for p in range(PARTS)]
        lhs = jnp.concatenate(rows, axis=0).astype(BF16)
        one = dot(lhs, y_ref[:, s * PC : (s + 1) * PC])
        total = one if total is None else total + one
    parts = []
    for p in range(PARTS):
        at = p * 2 * TP
        parts.append(total[at : at + TOK] + total[at + TP : at + TP + TOK])
    low = jnp.concatenate(parts[: PARTS // 2], axis=1)
    high = jnp.concatenate(parts[PARTS // 2 :], axis=1)
    first = parity == 0
    keep_ref[...] = jnp.where(first, res_ref[:, :half] + low, res_ref[:, half:] + high)
    send_ref[...] = jnp.where(first, high, low).astype(BF16)


def combine_call(y, mix, residual):
    return pl.pallas_call(
        combine_kernel,
        out_shape=[
            jax.ShapeDtypeStruct((TOK, D // 2), F32),
            jax.ShapeDtypeStruct((TOK, D // 2), BF16),
        ],
        compiler_params=pltpu.CompilerParams(vmem_limit_bytes=24 * MiB),
        cost_estimate=pl.CostEstimate(flops=4 * 10**8, bytes_accessed=10**6, transcendentals=0),
        name="combine",
    )(y, mix, residual)


def final_kernel(keep_ref, got_ref, out_ref):
    total = keep_ref[...] + got_ref[...].astype(F32)
    steps = [total[t * R : (t + 1) * R] for t in range(T)]
    out_ref[...] = jnp.stack(steps, axis=1).astype(BF16)


def final_call(keep, got):
    return pl.pallas_call(
        final_kernel,
        out_shape=jax.ShapeDtypeStruct((R, T, D // 2), BF16),
        name="final",
    )(keep, got)


def local(
    hidden_in,
    new_queries,
    new_keys,
    new_values,
    out_gate,
    decay_logit,
    write_logit,
    decay_scale,
    decay_bias,
    head_gain,
    out_projection,
    norm_gain,
    expert_ids,
    route_weight,
    gate_weight,
    up_weight,
    down_weight,
    old_state,
):
    pick, mix = table_call(expert_ids, route_weight)
    own, send, keys, updates, factor = core_call(
        new_queries,
        new_keys,
        new_values,
        out_gate,
        decay_logit,
        write_logit,
        decay_scale.reshape(1, -1),
        decay_bias.reshape(1, -1),
        head_gain.reshape(1, -1),
        hidden_in,
        old_state,
        out_projection,
    )
    swap = [(0, 1), (1, 0)]
    got = lax.ppermute(send, "hd", swap)
    residual, outbound = dispatch_call(own, got, norm_gain.reshape(1, -1), pick)
    shape = (CHIPS, PARTS, SLOTS * PC)
    arrived = lax.all_to_all(outbound.reshape(shape), "ep", 0, 0, tiled=True)
    new_state = state_call(old_state, keys, updates, factor)
    produced = expert_call(arrived.reshape(outbound.shape), gate_weight, up_weight, down_weight)
    returned = lax.all_to_all(produced.reshape(shape), "ep", 0, 0, tiled=True)
    keep, give = combine_call(returned.reshape(outbound.shape), mix, residual)
    output_rows = final_call(keep, lax.ppermute(give, "hd", swap))
    return (output_rows, new_state)


def solution(mesh):
    in_specs = (
        P("ep", None, None),
        P("ep", None, "hd", None),
        P("ep", None, "hd", None),
        P("ep", None, "hd", None),
        P("ep", None, "hd", None),
        P("ep", None, "hd"),
        P("ep", None, "hd"),
        P("hd"),
        P("hd"),
        P(),
        P("hd", None),
        P(),
        P("ep", None, None),
        P("ep", None, None),
        P(("ep", "hd"), None, None),
        P(("ep", "hd"), None, None),
        P(("ep", "hd"), None, None),
        P("ep", "hd", None, None),
    )
    out_specs = (P("ep", None, "hd"), P("ep", "hd", None, None))
    return jax.shard_map(local, mesh=mesh, in_specs=in_specs, out_specs=out_specs, check_vma=False)
```

profile of v0, /device:TPU:1, one launch (start us, length us, event | category | flops | bytes accessed | tf_op | source)
XLA Modules:
  0.0 84.7 jit_solution(13109984627181660701)
XLA Ops:
  0.6 0.7 copy.20.a_ref
  1.3 0.7 copy.21.b_ref
  2.0 1.0 %copy.22.h_ref = bf16[8,3,2048]{2,1,0:T(4,128)(2,1)S(1)} copy(bf16[8,3,2048]{2,0,1:T(8,128)(2,1)} %param.18) | data formatting | bytes 196608 | tf_op args[0]
  3.0 3.4 %copy-done = f32[8,16,128,128]{3,2,1,0:T(8,128)S(1)} copy-done((f32[8,16,128,128]{3,2,1,0:T(8,128)S(1)}, f32[8,16,128,128]{3,2,1,0:T(8,128)}, u32[]{:S(2)}) %copy-start) | copy-done | bytes 8388632
  6.4 3.4 %copy-done.2 = bf16[2048,2048]{1,0:T(8,128)(2,1)S(1)} copy-done((bf16[2048,2048]{1,0:T(8,128)(2,1)S(1)}, bf16[2048,2048]{1,0:T(8,128)(2,1)}, u32[]{:S(2)}) %copy-start.2) | copy-done | bytes 8388632
  9.8 0.9 %copy-done.6 = bf16[8,3,16,128]{3,2,1,0:T(8,128)(2,1)S(1)} copy-done((bf16[8,3,16,128]{3,2,1,0:T(8,128)(2,1)S(1)}, bf16[8,3,16,128]{3,2,1,0:T(8,128)(2,1)}, u32[]{:S(2)}) %copy-start.6) | copy-done | bytes 98328
  10.7 0.9 %copy-done.7 = bf16[8,3,16,128]{3,2,1,0:T(8,128)(2,1)S(1)} copy-done((bf16[8,3,16,128]{3,2,1,0:T(8,128)(2,1)S(1)}, bf16[8,3,16,128]{3,2,1,0:T(8,128)(2,1)}, u32[]{:S(2)}) %copy-start.7) | copy-done | bytes 98328
  11.6 0.8 copy-done.9
  12.4 0.8 copy-done.10
  13.2 0.7 copy-done.12
  13.8 0.7 copy-done.13
  14.5 0.7 copy-done.14
  15.2 6.5 %core.1 = (f32[24,2048]{1,0:T(8,128)S(1)}, bf16[24,2048]{1,0:T(8,128)(2,1)S(1)}, f32[8,24,128]{2,1,0:T(8,128)S(1)}, f32[8,24,256]{2,1,0:T(8,128)S(1)}, f32[8,8,256]{2,1,0:T(8,128)S(1)}) custom-call(bf16[8,3,8,128]{3,2,1,0:T(8,128)(2,1)S(1)} %copy-done.9, bf16[8,3,8,128]{3,2,1,0:T(8,128)(2,1)S(1)} %copy-done.10, bf16[8,3,16,128]{3,2,1,0:T(8,128)(2,1)S(1)} %copy-done.6, ...), custom_call_target="tpu_custom_call" | custom-call | flops 1000000000 | bytes 17825792 | tf_op jit(solution)/shard_map/core/pallas_call | solution.py:137
  21.7 1.5 %collective-permute-start = (bf16[24,2048]{1,0:T(8,128)(2,1)S(1)}, bf16[24,2048]{1,0:T(8,128)(2,1)S(1)}, u32[]{:S(2)}, u32[]{:S(2)}) collective-permute-start(bf16[24,2048]{1,0:T(8,128)(2,1)S(1)} %get-tuple-element.14), channel_id=1, source_target_pairs={{0,1},{1,0},{2,3},{3,2},{4,5},{5,4},{6,7},{7,6},{8,9},{9,8},{10,11... | collective-permute-start | bytes 294920 | tf_op jit(solution)/shard_map/ppermute | solution.py:403
  23.2 1.0 %tables.1 = (bf16[3,512,256]{2,1,0:T(8,128)(2,1)S(1)}, bf16[3,64,512]{2,1,0:T(8,128)(2,1)S(1)}) custom-call(s32[8,3,10]{2,1,0:T(4,128)S(1)} %copy.23.ids_ref, f32[8,3,10]{2,1,0:T(4,128)S(1)} %copy.24.route_ref), custom_call_target="tpu_custom_call" | custom-call | flops 100000000 | bytes 1000000 | tf_op jit(solution)/shard_map/tables/pallas_call | solution.py:245
  24.7 26.4 %all_to_all.10 = bf16[64,8,768]{2,1,0:T(8,128)(2,1)S(1)} all-to-all(bf16[64,8,768]{2,1,0:T(8,128)(2,1)S(1)} %bitcast.11), channel_id=1, replica_groups=mesh['ep'=64,'hd'=2] {'ep'}, dimensions={0} | all-to-all | bytes 1572864 | tf_op jit(solution)/shard_map/all_to_all | solution.py:406
  51.1 1.7 %expert.1 = bf16[512,768]{1,0:T(8,128)(2,1)S(1)} custom-call(bf16[512,768]{1,0:T(8,128)(2,1)S(1)} %bitcast.8, bf16[1,2048,512]{2,1,0:T(8,128)(2,1)S(1)} %copy-done.3, bf16[1,2048,512]{2,1,0:T(8,128)(2,1)S(1)} %copy-done.4, bf16[1,512,2048]{2,1,0:T(8,128)(2,1)S(1)} %copy-done.5), custom_call_target="tpu_custom_call" | custom-call | flops 1200000000 | bytes 8000000 | tf_op jit(solution)/shard_map/expert/pallas_call | solution.py:308
  52.8 18.3 %all_to_all.11 = bf16[64,8,768]{2,1,0:T(8,128)(2,1)S(1)} all-to-all(bf16[64,8,768]{2,1,0:T(8,128)(2,1)S(1)} %bitcast.9), channel_id=1, replica_groups=mesh['ep'=64,'hd'=2] {'ep'}, dimensions={0} | all-to-all | bytes 1572864 | tf_op jit(solution)/shard_map/all_to_all | solution.py:409
  71.2 0.6 combine.1
  71.8 3.2 %collective-permute-start.1 = (bf16[24,1024]{1,0:T(8,128)(2,1)S(1)}, bf16[24,1024]{1,0:T(8,128)(2,1)S(1)}, u32[]{:S(2)}, u32[]{:S(2)}) collective-permute-start(bf16[24,1024]{1,0:T(8,128)(2,1)S(1)} %get-tuple-element.20), channel_id=1, source_target_pairs={{0,1},{1,0},{2,3},{3,2},{4,5},{5,4},{6,7},{7,6},{8,9},{9,8},{10,11... | collective-permute-start | bytes 147464 | tf_op jit(solution)/shard_map/ppermute | solution.py:411
  75.0 6.0 %state.1 = f32[8,16,128,128]{3,2,1,0:T(8,128)} custom-call(f32[8,16,128,128]{3,2,1,0:T(8,128)S(1)} %copy-done.1, f32[8,24,128]{2,1,0:T(8,128)S(1)} %get-tuple-element.21.k_ref, f32[8,24,256]{2,1,0:T(8,128)S(1)} %get-tuple-element.22.u_ref, f32[8,8,256]{2,1,0:T(8,128)S(1)} %get-tuple-element.23.f_ref), custom_call_target="tpu_custom_call" | custom-call | flops 1000000000 | bytes 17825792 | tf_op jit(solution)/shard_map/state/pallas_call | solution.py:193
  81.0 0.6 copy-done.15
  81.6 1.6 %final.1 = bf16[8,3,1024]{2,1,0:T(4,128)(2,1)} custom-call(f32[24,1024]{1,0:T(8,128)} %copy-done.8, bf16[24,1024]{1,0:T(8,128)(2,1)} %copy-done.15), custom_call_target="tpu_custom_call" | custom-call | tf_op jit(solution)/shard_map/final/pallas_call | solution.py:360
  83.2 1.5 %copy.25 = bf16[8,3,1024]{2,0,1:T(8,128)(2,1)} copy(bf16[8,3,1024]{2,1,0:T(4,128)(2,1)} %final.1) | data formatting | bytes 98304
  (31 shorter events, 0.6 us)
Async XLA Ops:
  3.0 3.4 %copy-start = (f32[8,16,128,128]{3,2,1,0:T(8,128)S(1)}, f32[8,16,128,128]{3,2,1,0:T(8,128)}, u32[]{:S(2)}) copy-start(f32[8,16,128,128]{3,2,1,0:T(8,128)} %s_ref.3) | copy-start | bytes 25165828
  6.4 3.4 %copy-start.2 = (bf16[2048,2048]{1,0:T(8,128)(2,1)S(1)}, bf16[2048,2048]{1,0:T(8,128)(2,1)}, u32[]{:S(2)}) copy-start(bf16[2048,2048]{1,0:T(8,128)(2,1)} %w_ref.1) | copy-start | bytes 25165828
  9.8 0.9 %copy-start.6 = (bf16[8,3,16,128]{3,2,1,0:T(8,128)(2,1)S(1)}, bf16[8,3,16,128]{3,2,1,0:T(8,128)(2,1)}, u32[]{:S(2)}) copy-start(bf16[8,3,16,128]{3,2,1,0:T(8,128)(2,1)} %v_ref.1) | copy-start | bytes 294916
  10.7 0.9 %copy-start.7 = (bf16[8,3,16,128]{3,2,1,0:T(8,128)(2,1)S(1)}, bf16[8,3,16,128]{3,2,1,0:T(8,128)(2,1)}, u32[]{:S(2)}) copy-start(bf16[8,3,16,128]{3,2,1,0:T(8,128)(2,1)} %g_ref.1) | copy-start | bytes 294916
  11.6 0.8 copy-start.9
  12.4 0.8 copy-start.10
  13.2 0.7 copy-start.12
  13.8 0.7 copy-start.13
  14.5 0.7 copy-start.14
  15.1 8.1 %copy-start.16 = (s32[8,3,10]{2,0,1:T(8,128)S(1)}, s32[8,3,10]{2,0,1:T(8,128)}, u32[]{:S(2)}) copy-start(s32[8,3,10]{2,0,1:T(8,128)} %param.30) | copy-start | bytes 2884
  15.1 8.1 %copy-start.17 = (f32[8,3,10]{2,0,1:T(8,128)S(1)}, f32[8,3,10]{2,0,1:T(8,128)}, u32[]{:S(2)}) copy-start(f32[8,3,10]{2,0,1:T(8,128)} %param.31) | copy-start | bytes 2884
  15.1 9.0 %copy-start.11 = (f32[2048]{0:T(1024)S(1)}, f32[2048]{0:T(1024)}, u32[]{:S(2)}) copy-start(f32[2048]{0:T(1024)} %param.29) | copy-start | bytes 24580
  15.1 35.9 %copy-start.3 = (bf16[1,2048,512]{2,1,0:T(8,128)(2,1)S(1)}, bf16[1,2048,512]{2,1,0:T(8,128)(2,1)}, u32[]{:S(2)}) copy-start(bf16[1,2048,512]{2,1,0:T(8,128)(2,1)} %gate_ref.1) | copy-start | bytes 6291460
  15.1 35.9 %copy-start.4 = (bf16[1,2048,512]{2,1,0:T(8,128)(2,1)S(1)}, bf16[1,2048,512]{2,1,0:T(8,128)(2,1)}, u32[]{:S(2)}) copy-start(bf16[1,2048,512]{2,1,0:T(8,128)(2,1)} %up_ref.1) | copy-start | bytes 6291460
  15.1 35.9 %copy-start.5 = (bf16[1,512,2048]{2,1,0:T(8,128)(2,1)S(1)}, bf16[1,512,2048]{2,1,0:T(8,128)(2,1)}, u32[]{:S(2)}) copy-start(bf16[1,512,2048]{2,1,0:T(8,128)(2,1)} %down_ref.1) | copy-start | bytes 6291460
  21.7 53.3 %copy-start.1 = (f32[8,16,128,128]{3,2,1,0:T(8,128)S(1)}, f32[8,16,128,128]{3,2,1,0:T(8,128)}, u32[]{:S(2)}) copy-start(f32[8,16,128,128]{3,2,1,0:T(8,128)} %s_ref.3) | copy-start | bytes 25165828
  21.7 2.5 %collective-permute-start = (bf16[24,2048]{1,0:T(8,128)(2,1)S(1)}, bf16[24,2048]{1,0:T(8,128)(2,1)S(1)}, u32[]{:S(2)}, u32[]{:S(2)}) collective-permute-start(bf16[24,2048]{1,0:T(8,128)(2,1)S(1)} %get-tuple-element.14), channel_id=1, source_target_pairs={{0,1},{1,0},{2,3},{3,2},{4,5},{5,4},{6,7},{7,6},{8,9},{9,8},{10,11... | collective-permute-start | bytes 294920 | tf_op jit(solution)/shard_map/ppermute | solution.py:403
  71.8 9.2 %copy-start.8 = (f32[24,1024]{1,0:T(8,128)}, f32[24,1024]{1,0:T(8,128)S(1)}, u32[]{:S(2)}) copy-start(f32[24,1024]{1,0:T(8,128)S(1)} %get-tuple-element.19.keep_ref) | copy-start | bytes 294916
  71.8 9.2 %collective-permute-start.1 = (bf16[24,1024]{1,0:T(8,128)(2,1)S(1)}, bf16[24,1024]{1,0:T(8,128)(2,1)S(1)}, u32[]{:S(2)}, u32[]{:S(2)}) collective-permute-start(bf16[24,1024]{1,0:T(8,128)(2,1)S(1)} %get-tuple-element.20), channel_id=1, source_target_pairs={{0,1},{1,0},{2,3},{3,2},{4,5},{5,4},{6,7},{7,6},{8,9},{9,8},{10,11... | collective-permute-start | bytes 147464 | tf_op jit(solution)/shard_map/ppermute | solution.py:411
  81.0 0.6 copy-start.15
where the time goes:
time: 85.3 us; the launch traced here: 84.7 us
  blocking collectives  44.7 us (52%)
  Pallas kernels  17.9 us (21%)
  local copies, waits for them, and re-layouts  16.6 us (19%)
  starting transfers between devices  4.68 us (5%)
    all_to_all x1, blocking collectives, local(): arrived = lax.all_to_all(outbound.reshape(shape), 'ep', 0, 0, tiled=True)  26.4 us
    all_to_all x1, blocking collectives, local(): returned = lax.all_to_all(produced.reshape(shape), 'ep', 0, 0, tiled=True)  18.3 us
    unnamed x42, local copies, waits for them, and re-layouts  16.6 us
    pallas_call x1, Pallas kernels, core_call(): pl.pallas_call(core_kernel, grid=(HK,), in_specs=[whole(x) for x in small...  6.49 us
    pallas_call x1, Pallas kernels, state_call(): pl.pallas_call(state_kernel, grid=(HK,), in_specs=[pl.BlockSpec((R, 2, 12...  6 us
    ppermute x1, starting transfers between devices, local(): output_rows = final_call(keep, lax.ppermute(give, 'hd', swap))  3.18 us
    pallas_call x1, Pallas kernels, expert_call(): pl.pallas_call(expert_kernel, out_shape=jax.ShapeDtypeStruct(x.shape, BF1...  1.74 us
  transfers between devices with their start and end apart: 2, of which 0 were waited for; matrix products, arithmetic and copies ran while one was open for 0% of the time, Pallas kernels for 8%

commit v1 on v0

v1 whole, which is shorter than its diff:
```python
import jax
import jax.numpy as jnp
from jax import lax
from jax.experimental import pallas as pl
from jax.experimental.pallas import tpu as pltpu
from jax.sharding import PartitionSpec as P

EPSILON = 1e-06
F32 = jnp.float32
BF16 = jnp.bfloat16

R = 8
T = 3
TOK = R * T
HK = 8
D = 2048
FF = 512
SLOTS = 3
CHIPS = 64
PARTS = 8
PC = D // PARTS
TP = 32
MiB = 1 << 20
CORE_VMEM = 55
GROUP = 8
AHEAD = 6
FLUSH_FIRST = (0, 1)
FLUSH_NEXT = (2, 3, 4)
FLUSH_LAST = (5, 6, 7)


def dot(a, b, dims=((1,), (0,))):
    return lax.dot_general(a, b, (dims, ((), ())), preferred_element_type=F32)


def iota(shape, dim):
    return lax.broadcasted_iota(jnp.int32, shape, dim)


def core_kernel(
    q_hbm, k_hbm, v_hbm, g_hbm, a_hbm, b_hbm, scale_hbm, bias_hbm, gain_hbm, h_hbm, s_hbm, w_hbm,
    own_ref, send_ref, state_ref,
    q_in, k_in, v_in, g_in, a_in, b_in, scale_in, bias_in, gain_in, h_in, w_in,
    qs, ks, vs, gs, fs, bs, lhs, seen, acc, small_sem, s_sem, w_sem,
):
    small = [
        pltpu.make_async_copy(source, target, small_sem.at[i])
        for i, (source, target) in enumerate(
            (
                (q_hbm, q_in),
                (k_hbm, k_in),
                (a_hbm, a_in),
                (b_hbm, b_in),
                (scale_hbm, scale_in),
                (bias_hbm, bias_in),
                (gain_hbm, gain_in),
                (v_hbm, v_in),
                (g_hbm, g_in),
                (h_hbm, h_in),
            )
        )
    ]
    state_in = [
        pltpu.make_async_copy(
            s_hbm.at[:, pl.ds(2 * i, 2)], state_ref.at[:, pl.ds(2 * i, 2)], s_sem.at[i]
        )
        for i in range(HK)
    ]
    weight_in = [
        pltpu.make_async_copy(
            w_hbm.at[pl.ds(i * 256, 256)], w_in.at[pl.ds(i * 256, 256)], w_sem.at[i]
        )
        for i in range(HK)
    ]
    stream = state_in + weight_in
    for copy in small + stream[:AHEAD]:
        copy.start()
    for copy in small:
        copy.wait()

    def arrive(n):
        stream[n].wait()
        if n + AHEAD < len(stream):
            stream[n + AHEAD].start()

    for t in range(T):
        for r in range(R):
            rows = pl.ds(t * HK * R + r, HK, stride=R)
            qs[rows, :] = q_in[r, t].astype(F32)
            ks[rows, :] = k_in[r, t].astype(F32)
            v = v_in[r, t].astype(F32)
            g = g_in[r, t].astype(F32)
            for half in range(2):
                rows = pl.ds((2 * t + half) * HK * R + r, HK, stride=R)
                vs[rows, :] = v[half * HK : (half + 1) * HK]
                gs[rows, :] = g[half * HK : (half + 1) * HK]
    rate = -jnp.exp(scale_in[...])
    for t in range(T):
        x = a_in[t].astype(F32) + bias_in[...]
        soft = jnp.maximum(x, 0.0) + jnp.log1p(jnp.exp(-jnp.abs(x)))
        factor = jnp.exp(rate * soft)
        strength = 1.0 / (1.0 + jnp.exp(-b_in[t].astype(F32)))
        for h in range(2 * HK):
            rows = slice((t * 2 * HK + h) * R, (t * 2 * HK + h + 1) * R)
            fs[rows, :] = jnp.broadcast_to(factor[:, h : h + 1], (R, 128))
            bs[rows, :] = jnp.broadcast_to(strength[:, h : h + 1], (R, 128))
    q = qs[...]
    k = ks[...]
    q = q * lax.rsqrt(jnp.sum(q * q, axis=-1, keepdims=True) + EPSILON)
    k = k * lax.rsqrt(jnp.sum(k * k, axis=-1, keepdims=True) + EPSILON)
    each = HK * R
    qt = [q[t * each : (t + 1) * each] for t in range(T)]
    kt = [k[t * each : (t + 1) * each] for t in range(T)]
    row_of = iota((2 * TOK, 128), 0) % R
    for i in range(HK):
        at = slice(i * R, (i + 1) * R)
        kq = jnp.concatenate([x[at] for x in kt + qt], axis=0)
        for r in range(R):
            lhs[i, :, r * 128 : (r + 1) * 128] = jnp.where(row_of == r, kq, 0.0).astype(BF16)

    def pair(x, y):
        return jnp.sum(x * y, axis=-1, keepdims=True)

    kk21, kk31, kk32 = pair(kt[1], kt[0]), pair(kt[2], kt[0]), pair(kt[2], kt[1])
    qk = [[pair(qt[t], kt[s]) for s in range(t + 1)] for t in range(T)]

    def split(x):
        high = x.astype(BF16).astype(F32)
        return high, x - high

    gain = gain_in[...]
    lane_of = iota((128, 3 * TOK), 1) % R
    outs = []
    for first in range(0, HK, GROUP):
        group = range(first, first + GROUP)
        span = slice(first * R, (first + GROUP) * R)
        for i in group:
            arrive(i)
            state = jnp.concatenate(
                [state_ref[:, 2 * i + j].reshape(R * 128, 128).astype(BF16) for j in range(2)],
                axis=1,
            )
            both = dot(lhs[i], state)
            for part in range(2 * T):
                seen[part, i * R : (i + 1) * R, :] = both[part * R : (part + 1) * R]

        k21, k31, k32 = kk21[span], kk31[span], kk32[span]
        qks = [[x[span] for x in row] for row in qk]
        late = []
        done = []
        for j in range(2):

            def of_heads(ref):
                return [
                    jnp.concatenate(
                        [ref[pl.ds((t * 2 * HK + 2 * i + j) * R, R), :] for i in group], axis=0
                    )
                    for t in range(T)
                ]

            lanes = slice(j * 128, (j + 1) * 128)
            f, b, v, gate = of_heads(fs), of_heads(bs), of_heads(vs), of_heads(gs)
            recall = [seen[t, span, lanes] for t in range(T)]
            look = [seen[T + t, span, lanes] for t in range(T)]
            f01 = f[0] * f[1]
            f12 = f[1] * f[2]
            f012 = f01 * f[2]
            u0 = b[0] * (v[0] - f[0] * recall[0])
            u1 = b[1] * (v[1] - f01 * recall[1] - f[1] * k21 * u0)
            u2 = b[2] * (v[2] - f012 * recall[2] - f12 * k31 * u0 - f[2] * k32 * u1)
            c0 = f[0] * look[0] + qks[0][0] * u0
            c1 = f01 * look[1] + f[1] * qks[1][0] * u0 + qks[1][1] * u1
            c2 = f012 * look[2] + f12 * qks[2][0] * u0 + f[2] * qks[2][1] * u1 + qks[2][2] * u2
            late.append((f12 * u0, f[2] * u1, u2, f012))
            ready = []
            for t, c in enumerate((c0, c1, c2)):
                normed = c * lax.rsqrt(jnp.mean(c * c, axis=-1, keepdims=True) + EPSILON) * gain
                ready.append(normed * (gate[t] * (1.0 / (1.0 + jnp.exp(-gate[t])))))
            done.append(ready)

        for i in group:
            at = slice((i - first) * R, (i - first + 1) * R)
            outs.append(
                jnp.concatenate(
                    [jnp.concatenate([x[at] for x in done[j]], axis=0) for j in range(2)], axis=1
                ).astype(BF16)
            )
            key_high, key_low = split(
                jnp.concatenate([x[i * R : (i + 1) * R] for x in kt], axis=0)
            )
            keys = jnp.concatenate([key_high, key_low, key_high], axis=0).T
            update = jnp.concatenate(
                [jnp.concatenate([x[at] for x in late[j][:3]], axis=0) for j in range(2)], axis=1
            )
            up_high, up_low = split(update)
            update = jnp.concatenate([up_high, up_high, up_low], axis=0).astype(BF16)
            for r in range(R):
                added = dot(jnp.where(lane_of == r, keys, 0.0).astype(BF16), update)
                row = (i - first) * R + r
                for j in range(2):
                    state_ref[r, 2 * i + j] = (
                        state_ref[r, 2 * i + j] * late[j][3][row : row + 1]
                        + added[:, j * 128 : (j + 1) * 128]
                    )
    for i in range(HK):
        arrive(HK + i)
        part = dot(outs[i], w_in[i * 256 : (i + 1) * 256, :])
        if i == 0:
            acc[...] = part
        elif i < HK - 1:
            acc[...] += part
        else:
            total = acc[...] + part
            send_ref[...] = total.astype(BF16)
            own_ref[...] = total + h_in[...].reshape(TOK, D).astype(F32)


def core_call(*args):
    args = [pltpu.with_memory_space_constraint(x, pltpu.HBM) for x in args]
    landing = [pltpu.VMEM(x.shape, x.dtype) for x in args[:10] + args[11:]]
    state = args[10]
    return pl.pallas_call(
        core_kernel,
        in_specs=[pl.BlockSpec(memory_space=pl.ANY)] * len(args),
        out_specs=[pl.BlockSpec(memory_space=pltpu.VMEM)] * 3,
        out_shape=[
            pltpu.VMEM((TOK, D), F32),
            pltpu.VMEM((TOK, D), BF16),
            pltpu.VMEM(state.shape, F32),
        ],
        scratch_shapes=landing
        + [pltpu.VMEM((HK * TOK, 128), F32)] * 2
        + [pltpu.VMEM((2 * HK * TOK, 128), F32)] * 4
        + [
            pltpu.VMEM((HK, 2 * TOK, R * 128), BF16),
            pltpu.VMEM((2 * T, HK * R, 256), F32),
            pltpu.VMEM((TOK, D), F32),
            pltpu.SemaphoreType.DMA((10,)),
            pltpu.SemaphoreType.DMA((HK,)),
            pltpu.SemaphoreType.DMA((HK,)),
        ],
        compiler_params=pltpu.CompilerParams(vmem_limit_bytes=CORE_VMEM * MiB),
        cost_estimate=pl.CostEstimate(flops=10**9, bytes_accessed=17 * MiB, transcendentals=10**5),
        name="core",
    )(*args)


def flush(state_ref, out_ref, sem, chunks):
    copies = []
    for n, i in enumerate(chunks):
        part = pl.ds(2 * i, 2)
        copies.append(pltpu.make_async_copy(state_ref.at[:, part], out_ref.at[:, part], sem.at[n]))
    for copy in copies:
        copy.start()
    return copies


def table_kernel(ids_ref, route_ref, state_ref, pick_ref, mix_ref, out_ref, sem):
    copies = flush(state_ref, out_ref, sem, FLUSH_FIRST)
    parity = lax.axis_index("hd")
    ids = ids_ref[...].reshape(TOK, -1)
    route = route_ref[...].reshape(TOK, -1)
    mixing = route / jnp.sum(route, axis=1, keepdims=True)
    expert = iota((TOK, CHIPS), 1) * 2 + parity
    named = jnp.zeros((TOK, CHIPS), F32)
    weight = jnp.zeros((TOK, CHIPS), F32)
    for c in range(ids.shape[1]):
        hit = ids[:, c : c + 1] == expert
        named = jnp.where(hit, 1.0, named)
        weight = jnp.where(hit, mixing[:, c : c + 1], weight)
    earlier = (iota((TOK, TOK), 0) > iota((TOK, TOK), 1)).astype(F32)
    rank = dot(earlier.astype(BF16), named.astype(BF16))
    rows = CHIPS * PARTS
    pad = jnp.zeros((TP - TOK, CHIPS), F32)
    spread = (iota((rows, CHIPS), 0) // PARTS == iota((rows, CHIPS), 1)).astype(F32).astype(BF16)
    across = (iota((CHIPS, rows), 1) // PARTS == iota((CHIPS, rows), 0)).astype(F32).astype(BF16)
    tile = (iota((TP, PARTS * TP), 1) % TP == iota((TP, PARTS * TP), 0)).astype(F32).astype(BF16)
    keep = iota((rows, PARTS * TP), 0) % PARTS == iota((rows, PARTS * TP), 1) // TP
    for s in range(SLOTS):
        here = jnp.where((named > 0.5) & (jnp.abs(rank - s) < 0.5), 1.0, 0.0)
        chosen = jnp.concatenate([here, pad], axis=0)
        tiled = dot(chosen.astype(BF16), tile, ((0,), (0,)))
        full = dot(spread, tiled.astype(BF16))
        pick_ref[s] = jnp.where(keep, full, 0.0).astype(BF16)
        share = jnp.concatenate([weight * here, pad], axis=0)
        high = share.astype(BF16).astype(F32)
        parts = jnp.concatenate([high, share - high], axis=0).astype(BF16)
        mix_ref[s] = dot(parts, across).astype(BF16)
    for copy in copies:
        copy.wait()


IN_VMEM = pl.BlockSpec(memory_space=pltpu.VMEM)
AS_IS = pl.BlockSpec(memory_space=pl.ANY)


def table_call(ids, route, state):
    return pl.pallas_call(
        table_kernel,
        in_specs=[IN_VMEM] * 2 + [AS_IS],
        out_specs=[IN_VMEM] * 2 + [AS_IS],
        out_shape=[
            jax.ShapeDtypeStruct((SLOTS, CHIPS * PARTS, PARTS * TP), BF16),
            jax.ShapeDtypeStruct((SLOTS, 2 * TP, CHIPS * PARTS), BF16),
            pltpu.HBM(state.shape, F32),
        ],
        scratch_shapes=[pltpu.SemaphoreType.DMA((len(FLUSH_FIRST),))],
        compiler_params=pltpu.CompilerParams(vmem_limit_bytes=16 * MiB),
        cost_estimate=pl.CostEstimate(flops=10**8, bytes_accessed=10**6, transcendentals=0),
        name="tables",
    )(ids, route, pltpu.with_memory_space_constraint(state, pltpu.VMEM))


def dispatch_kernel(own_ref, got_ref, gain_ref, pick_ref, res_ref, out_ref):
    residual = own_ref[...] + got_ref[...].astype(F32)
    res_ref[...] = residual
    scale = lax.rsqrt(jnp.mean(residual * residual, axis=1, keepdims=True) + EPSILON)
    normed = residual * scale * gain_ref[...]
    pad = jnp.zeros((TP - TOK, PC), F32)
    pieces = []
    for p in range(PARTS):
        pieces += [normed[:, p * PC : (p + 1) * PC], pad]
    stacked = jnp.concatenate(pieces, axis=0).astype(BF16)
    for s in range(SLOTS):
        out_ref[:, s * PC : (s + 1) * PC] = dot(pick_ref[s], stacked).astype(BF16)


def dispatch_call(own, got, gain, pick):
    return pl.pallas_call(
        dispatch_kernel,
        out_shape=[
            jax.ShapeDtypeStruct((TOK, D), F32),
            jax.ShapeDtypeStruct((CHIPS * PARTS, SLOTS * PC), BF16),
        ],
        compiler_params=pltpu.CompilerParams(vmem_limit_bytes=16 * MiB),
        cost_estimate=pl.CostEstimate(flops=2 * 10**8, bytes_accessed=2 * 10**6, transcendentals=0),
        name="dispatch",
    )(own, got, gain, pick)


def expert_kernel(
    x_ref, gate_ref, up_ref, down_ref, state_ref, held_ref, y_ref, out_ref, wide, sem
):
    copies = flush(state_ref, out_ref, sem, FLUSH_NEXT)
    chunks = SLOTS * PC // 128
    for c in range(chunks):
        wide[c] = x_ref[:, c * 128 : (c + 1) * 128].astype(F32)
    gate = jnp.zeros((SLOTS * CHIPS, FF), F32)
    up = jnp.zeros((SLOTS * CHIPS, FF), F32)
    for p in range(PARTS):
        rows = [wide[c, pl.ds(p, CHIPS, stride=PARTS), :] for c in range(chunks)]
        x = jnp.concatenate(
            [jnp.concatenate(rows[0::2], axis=0), jnp.concatenate(rows[1::2], axis=0)], axis=1
        ).astype(BF16)
        gate += dot(x, gate_ref[0, p * PC : (p + 1) * PC, :])
        up += dot(x, up_ref[0, p * PC : (p + 1) * PC, :])
    activated = (gate * (1.0 / (1.0 + jnp.exp(-gate))) * up).astype(BF16)
    for p in range(PARTS):
        y = dot(activated, down_ref[0, :, p * PC : (p + 1) * PC])
        for c in range(chunks):
            at, side = c // 2 * CHIPS, c % 2 * 128
            wide[c, pl.ds(p, CHIPS, stride=PARTS), :] = y[at : at + CHIPS, side : side + 128]
    for c in range(chunks):
        y_ref[:, c * 128 : (c + 1) * 128] = wide[c].astype(BF16)
    for copy in copies:
        copy.wait()


def expert_call(x, gate, up, down, state, held):
    return pl.pallas_call(
        expert_kernel,
        in_specs=[IN_VMEM] * 4 + [AS_IS] * 2,
        out_specs=[IN_VMEM, AS_IS],
        out_shape=[jax.ShapeDtypeStruct(x.shape, BF16), pltpu.HBM(state.shape, F32)],
        input_output_aliases={5: 1},
        scratch_shapes=[
            pltpu.VMEM((x.shape[1] // 128, x.shape[0], 128), F32),
            pltpu.SemaphoreType.DMA((len(FLUSH_NEXT),)),
        ],
        compiler_params=pltpu.CompilerParams(vmem_limit_bytes=24 * MiB),
        cost_estimate=pl.CostEstimate(
            flops=12 * 10**8, bytes_accessed=8 * 10**6, transcendentals=10**5
        ),
        name="expert",
    )(
        x,
        gate,
        up,
        down,
        pltpu.with_memory_space_constraint(state, pltpu.VMEM),
        pltpu.with_memory_space_constraint(held, pltpu.HBM),
    )


def combine_kernel(y_ref, mix_ref, res_ref, keep_ref, send_ref):
    parity = lax.axis_index("hd")
    part_of = iota((2 * TP, CHIPS * PARTS), 1) % PARTS
    half = D // 2
    total = None
    for s in range(SLOTS):
        mix = mix_ref[s].astype(F32)
        rows = [jnp.where(part_of == p, mix, 0.0) for p in range(PARTS)]
        lhs = jnp.concatenate(rows, axis=0).astype(BF16)
        one = dot(lhs, y_ref[:, s * PC : (s + 1) * PC])
        total = one if total is None else total + one
    parts = []
    for p in range(PARTS):
        at = p * 2 * TP
        parts.append(total[at : at + TOK] + total[at + TP : at + TP + TOK])
    low = jnp.concatenate(parts[: PARTS // 2], axis=1)
    high = jnp.concatenate(parts[PARTS // 2 :], axis=1)
    first = parity == 0
    keep_ref[...] = jnp.where(first, res_ref[:, :half] + low, res_ref[:, half:] + high)
    send_ref[...] = jnp.where(first, high, low).astype(BF16)


def combine_call(y, mix, residual):
    return pl.pallas_call(
        combine_kernel,
        out_shape=[
            jax.ShapeDtypeStruct((TOK, D // 2), F32),
            jax.ShapeDtypeStruct((TOK, D // 2), BF16),
        ],
        compiler_params=pltpu.CompilerParams(vmem_limit_bytes=24 * MiB),
        cost_estimate=pl.CostEstimate(flops=4 * 10**8, bytes_accessed=10**6, transcendentals=0),
        name="combine",
    )(y, mix, residual)


def last_kernel(state_ref, held_ref, out_ref, sem):
    for copy in flush(state_ref, out_ref, sem, FLUSH_LAST):
        copy.wait()


def last_call(state, held):
    return pl.pallas_call(
        last_kernel,
        in_specs=[AS_IS] * 2,
        out_specs=AS_IS,
        out_shape=pltpu.HBM(state.shape, F32),
        input_output_aliases={1: 0},
        scratch_shapes=[pltpu.SemaphoreType.DMA((len(FLUSH_LAST),))],
        compiler_params=pltpu.CompilerParams(vmem_limit_bytes=4 * MiB),
        cost_estimate=pl.CostEstimate(flops=0, bytes_accessed=6 * MiB, transcendentals=0),
        name="last",
    )(
        pltpu.with_memory_space_constraint(state, pltpu.VMEM),
        pltpu.with_memory_space_constraint(held, pltpu.HBM),
    )


def local(
    hidden_in,
    new_queries,
    new_keys,
    new_values,
    out_gate,
    decay_logit,
    write_logit,
    decay_scale,
    decay_bias,
    head_gain,
    out_projection,
    norm_gain,
    expert_ids,
    route_weight,
    gate_weight,
    up_weight,
    down_weight,
    old_state,
):
    def by_step(x):
        return jnp.transpose(x, (1, 0, 2))

    own, send, fresh = core_call(
        new_queries,
        new_keys,
        new_values,
        out_gate,
        by_step(decay_logit),
        by_step(write_logit),
        decay_scale.reshape(1, -1),
        decay_bias.reshape(1, -1),
        head_gain.reshape(1, -1),
        by_step(hidden_in),
        old_state,
        out_projection,
    )
    swap = [(0, 1), (1, 0)]
    got = lax.ppermute(send, "hd", swap)
    pick, mix, held = table_call(by_step(expert_ids), by_step(route_weight), fresh)
    residual, outbound = dispatch_call(own, got, norm_gain.reshape(1, -1), pick)
    shape = (CHIPS, PARTS, SLOTS * PC)
    arrived = lax.all_to_all(outbound.reshape(shape), "ep", 0, 0, tiled=True)
    produced, held = expert_call(
        arrived.reshape(outbound.shape), gate_weight, up_weight, down_weight, fresh, held
    )
    returned = lax.all_to_all(produced.reshape(shape), "ep", 0, 0, tiled=True)
    keep, give = combine_call(returned.reshape(outbound.shape), mix, residual)
    got = lax.ppermute(give, "hd", swap)
    new_state = last_call(fresh, held)
    total = keep + got.astype(F32)
    output_rows = by_step(total.astype(BF16).reshape(T, R, -1))
    return (output_rows, new_state)


def solution(mesh):
    in_specs = (
        P("ep", None, None),
        P("ep", None, "hd", None),
        P("ep", None, "hd", None),
        P("ep", None, "hd", None),
        P("ep", None, "hd", None),
        P("ep", None, "hd"),
        P("ep", None, "hd"),
        P("hd"),
        P("hd"),
        P(),
        P("hd", None),
        P(),
        P("ep", None, None),
        P("ep", None, None),
        P(("ep", "hd"), None, None),
        P(("ep", "hd"), None, None),
        P(("ep", "hd"), None, None),
        P("ep", "hd", None, None),
    )
    out_specs = (P("ep", None, "hd"), P("ep", "hd", None, None))
    return jax.shard_map(local, mesh=mesh, in_specs=in_specs, out_specs=out_specs, check_vma=False)
```

time: 85.3 us -> 66.2 us (0.78)
  local copies, waits for them, and re-layouts: 16.6 us -> 0.03 us
  Pallas kernels: 17.9 us -> 15.3 us
    unnamed x42 -> x12, local copies, waits for them, and re-layouts: 16.6 us -> 0.03 us
    pallas_call x5 -> x4, Pallas kernels: 16.8 us -> 14.2 us  [the longest x1 8.68 us: core_call(): pl.pallas_call(core_kernel, in_specs=[pl.BlockSpec(memory_space=pl.ANY)]...]
  transfers between devices with their start and end apart: 2 -> 2, of which waited for: 0 -> 0; matrix products, arithmetic and copies ran while one was open for 0% -> 0% of each run, Pallas kernels for 8% -> 5%
where the time goes in v1:
time: 66.2 us; the launch traced here: 66 us
  blocking collectives  44.5 us (67%)
  Pallas kernels  15.3 us (23%)
  starting transfers between devices  4.71 us (7%)
  between operations  0.76 us (1%)
    all_to_all x1, blocking collectives, local(): arrived = lax.all_to_all(outbound.reshape(shape), 'ep', 0, 0, tiled=True)  26.5 us
    all_to_all x1, blocking collectives, local(): returned = lax.all_to_all(produced.reshape(shape), 'ep', 0, 0, tiled=True)  18.1 us
    pallas_call x1, Pallas kernels, core_call(): pl.pallas_call(core_kernel, in_specs=[pl.BlockSpec(memory_space=pl.ANY)]...  8.68 us
    ppermute x1, starting transfers between devices, local(): got = lax.ppermute(give, 'hd', swap)  3.21 us
    pallas_call x1, Pallas kernels, expert_call(): pl.pallas_call(expert_kernel, in_specs=[IN_VMEM] * 4 + [AS_IS] * 2, out_s...  2.53 us
    pallas_call x1, Pallas kernels, last_call(): pl.pallas_call(last_kernel, in_specs=[AS_IS] * 2, out_specs=AS_IS, out_sh...  1.68 us
    ppermute x1, starting transfers between devices, local(): got = lax.ppermute(send, 'hd', swap)  1.5 us
    pallas_call x1, Pallas kernels, table_call(): pl.pallas_call(table_kernel, in_specs=[IN_VMEM] * 2 + [AS_IS], out_specs=...  1.34 us
  transfers between devices with their start and end apart: 2, of which 0 were waited for; matrix products, arithmetic and copies ran while one was open for 0% of the time, Pallas kernels for 5%

profile of v1, /device:TPU:1, one launch (start us, length us, event | category | flops | bytes accessed | tf_op | source)
XLA Modules:
  0.0 66.0 jit_solution(8771473261147689196)
XLA Ops:
  0.6 0.0 copy-start.3
  0.6 0.0 copy-start.4
  0.7 8.7 %core.1 = (f32[24,2048]{1,0:T(8,128)S(1)}, bf16[24,2048]{1,0:T(8,128)(2,1)S(1)}, f32[8,16,128,128]{3,2,1,0:T(8,128)S(1)}) custom-call(bf16[8,3,8,128]{3,2,1,0:T(8,128)(2,1)} %q_hbm.1, bf16[8,3,8,128]{3,2,1,0:T(8,128)(2,1)} %k_hbm.1, bf16[8,3,16,128]{3,2,1,0:T(8,128)(2,1)} %v_hbm.1, bf16[8,3,16,128]{3,2,1,0:T(8,128)(2,1)} %g_hbm.1, ...), custom_call_target="tpu_custom_call" | custom-call | flops 1000000000 | bytes 17825792 | tf_op jit(solution)/shard_map/core/pallas_call | solution.py:222
  9.3 0.0 copy-start.5
  9.4 0.0 copy-start
  9.4 0.0 copy-start.1
  9.4 0.0 copy-start.2
  9.4 1.5 %collective-permute-start = (bf16[24,2048]{1,0:T(8,128)(2,1)S(1)}, bf16[24,2048]{1,0:T(8,128)(2,1)S(1)}, u32[]{:S(2)}, u32[]{:S(2)}) collective-permute-start(bf16[24,2048]{1,0:T(8,128)(2,1)S(1)} %get-tuple-element.15), channel_id=1, source_target_pairs={{0,1},{1,0},{2,3},{3,2},{4,5},{5,4},{6,7},{7,6},{8,9},{9,8},{10,11... | collective-permute-start | bytes 294920 | tf_op jit(solution)/shard_map/ppermute | solution.py:490
  10.9 0.0 copy-done.3
  10.9 0.0 copy-done.4
  10.9 1.3 %tables.1 = (bf16[3,512,256]{2,1,0:T(8,128)(2,1)S(1)}, bf16[3,64,512]{2,1,0:T(8,128)(2,1)S(1)}, f32[8,16,128,128]{3,2,1,0:T(8,128)}) custom-call(s32[3,8,10]{2,1,0:T(8,128)S(1)} %bitcast.21, f32[3,8,10]{2,1,0:T(8,128)S(1)} %bitcast.22, f32[8,16,128,128]{3,2,1,0:T(8,128)S(1)} %get-tuple-element.16.state_ref), custom_call_target="tpu_custom_call" | custom-call | flops 100000000 | bytes 1000000 | tf_op jit(solution)/shard_map/tables/pallas_call | solution.py:298
  12.2 0.0 collective-permute-done.got_ref
  12.3 0.0 copy-done.5
  12.3 0.5 dispatch.1
  12.8 26.5 %all_to_all.10 = bf16[64,8,768]{2,1,0:T(8,128)(2,1)S(1)} all-to-all(bf16[64,8,768]{2,1,0:T(8,128)(2,1)S(1)} %bitcast.19), channel_id=1, replica_groups=mesh['ep'=64,'hd'=2] {'ep'}, dimensions={0} | all-to-all | bytes 1572864 | tf_op jit(solution)/shard_map/all_to_all | solution.py:494
  39.2 0.0 copy-done
  39.2 0.0 copy-done.1
  39.2 2.5 %expert.1 = (bf16[512,768]{1,0:T(8,128)(2,1)S(1)}, f32[8,16,128,128]{3,2,1,0:T(8,128)}) custom-call(bf16[512,768]{1,0:T(8,128)(2,1)S(1)} %bitcast.17, bf16[1,2048,512]{2,1,0:T(8,128)(2,1)S(1)} %copy-done, bf16[1,2048,512]{2,1,0:T(8,128)(2,1)S(1)} %copy-done.1, bf16[1,512,2048]{2,1,0:T(8,128)(2,1)S(1)} %copy-done.2, ...), custom_call_target="tpu_custom_call", output_to_operand_aliasing={{1}: (5, {})} | custom-call | flops 1200000000 | bytes 8000000 | tf_op jit(solution)/shard_map/expert/pallas_call | solution.py:370
  41.8 18.1 %all_to_all.11 = bf16[64,8,768]{2,1,0:T(8,128)(2,1)S(1)} all-to-all(bf16[64,8,768]{2,1,0:T(8,128)(2,1)S(1)} %bitcast.20), channel_id=1, replica_groups=mesh['ep'=64,'hd'=2] {'ep'}, dimensions={0} | all-to-all | bytes 1572864 | tf_op jit(solution)/shard_map/all_to_all | solution.py:498
  59.8 0.6 combine.1
  60.4 3.2 %collective-permute-start.1 = (bf16[24,1024]{1,0:T(8,128)(2,1)S(1)}, bf16[24,1024]{1,0:T(8,128)(2,1)S(1)}, u32[]{:S(2)}, u32[]{:S(2)}) collective-permute-start(bf16[24,1024]{1,0:T(8,128)(2,1)S(1)} %get-tuple-element.24), channel_id=1, source_target_pairs={{0,1},{1,0},{2,3},{3,2},{4,5},{5,4},{6,7},{7,6},{8,9},{9,8},{10,11... | collective-permute-start | bytes 147464 | tf_op jit(solution)/shard_map/ppermute | solution.py:500
  63.7 1.7 %last.1 = f32[8,16,128,128]{3,2,1,0:T(8,128)} custom-call(f32[8,16,128,128]{3,2,1,0:T(8,128)S(1)} %get-tuple-element.16.state_ref, f32[8,16,128,128]{3,2,1,0:T(8,128)} %get-tuple-element.25.held_ref), custom_call_target="tpu_custom_call", output_to_operand_aliasing={{}: (1, {})} | custom-call | bytes 6291456 | tf_op jit(solution)/shard_map/last/pallas_call | solution.py:436
  65.3 0.0 collective-permute-done.1
  65.4 0.6 fusion
  (1 shorter events, 0.0 us)
Async XLA Ops:
  0.6 10.3 %copy-start.3 = (s32[8,3,10]{2,0,1:T(8,128)S(1)}, s32[8,3,10]{2,0,1:T(8,128)}, u32[]{:S(2)}) copy-start(s32[8,3,10]{2,0,1:T(8,128)} %param.30) | copy-start | bytes 2884
  0.6 10.3 %copy-start.4 = (f32[8,3,10]{2,0,1:T(8,128)S(1)}, f32[8,3,10]{2,0,1:T(8,128)}, u32[]{:S(2)}) copy-start(f32[8,3,10]{2,0,1:T(8,128)} %param.31) | copy-start | bytes 2884
  9.3 2.9 %copy-start.5 = (f32[2048]{0:T(1024)S(1)}, f32[2048]{0:T(1024)}, u32[]{:S(2)}) copy-start(f32[2048]{0:T(1024)} %param.29) | copy-start | bytes 24580
  9.4 29.9 %copy-start = (bf16[1,2048,512]{2,1,0:T(8,128)(2,1)S(1)}, bf16[1,2048,512]{2,1,0:T(8,128)(2,1)}, u32[]{:S(2)}) copy-start(bf16[1,2048,512]{2,1,0:T(8,128)(2,1)} %gate_ref.1) | copy-start | bytes 6291460
  9.4 29.9 %copy-start.1 = (bf16[1,2048,512]{2,1,0:T(8,128)(2,1)S(1)}, bf16[1,2048,512]{2,1,0:T(8,128)(2,1)}, u32[]{:S(2)}) copy-start(bf16[1,2048,512]{2,1,0:T(8,128)(2,1)} %up_ref.1) | copy-start | bytes 6291460
  9.4 29.9 %copy-start.2 = (bf16[1,512,2048]{2,1,0:T(8,128)(2,1)S(1)}, bf16[1,512,2048]{2,1,0:T(8,128)(2,1)}, u32[]{:S(2)}) copy-start(bf16[1,512,2048]{2,1,0:T(8,128)(2,1)} %down_ref.1) | copy-start | bytes 6291460
  9.4 2.9 %collective-permute-start = (bf16[24,2048]{1,0:T(8,128)(2,1)S(1)}, bf16[24,2048]{1,0:T(8,128)(2,1)S(1)}, u32[]{:S(2)}, u32[]{:S(2)}) collective-permute-start(bf16[24,2048]{1,0:T(8,128)(2,1)S(1)} %get-tuple-element.15), channel_id=1, source_target_pairs={{0,1},{1,0},{2,3},{3,2},{4,5},{5,4},{6,7},{7,6},{8,9},{9,8},{10,11... | collective-permute-start | bytes 294920 | tf_op jit(solution)/shard_map/ppermute | solution.py:490
  60.4 4.9 %collective-permute-start.1 = (bf16[24,1024]{1,0:T(8,128)(2,1)S(1)}, bf16[24,1024]{1,0:T(8,128)(2,1)S(1)}, u32[]{:S(2)}, u32[]{:S(2)}) collective-permute-start(bf16[24,1024]{1,0:T(8,128)(2,1)S(1)} %get-tuple-element.24), channel_id=1, source_target_pairs={{0,1},{1,0},{2,3},{3,2},{4,5},{5,4},{6,7},{7,6},{8,9},{9,8},{10,11... | collective-permute-start | bytes 147464 | tf_op jit(solution)/shard_map/ppermute | solution.py:500

commit v2 on v1

--- a/solution.py
+++ b/solution.py
@@ -22,8 +22,8 @@
 TP = 32
 MiB = 1 << 20
 CORE_VMEM = 55
-GROUP = 8
-AHEAD = 6
+GROUP = 2
+AHEAD = 3
 FLUSH_FIRST = (0, 1)
 FLUSH_NEXT = (2, 3, 4)
 FLUSH_LAST = (5, 6, 7)
@@ -41,7 +41,7 @@
     q_hbm, k_hbm, v_hbm, g_hbm, a_hbm, b_hbm, scale_hbm, bias_hbm, gain_hbm, h_hbm, s_hbm, w_hbm,
     own_ref, send_ref, state_ref,
     q_in, k_in, v_in, g_in, a_in, b_in, scale_in, bias_in, gain_in, h_in, w_in,
-    qs, ks, vs, gs, fs, bs, lhs, seen, acc, small_sem, s_sem, w_sem,
+    qs, ks, vs, gs, fs, bs, lhs, seen, acc, small_sem, stream_sem,
 ):
     small = [
         pltpu.make_async_copy(source, target, small_sem.at[i])
@@ -60,19 +60,14 @@
             )
         )
     ]
-    state_in = [
-        pltpu.make_async_copy(
-            s_hbm.at[:, pl.ds(2 * i, 2)], state_ref.at[:, pl.ds(2 * i, 2)], s_sem.at[i]
-        )
-        for i in range(HK)
-    ]
-    weight_in = [
-        pltpu.make_async_copy(
-            w_hbm.at[pl.ds(i * 256, 256)], w_in.at[pl.ds(i * 256, 256)], w_sem.at[i]
-        )
-        for i in range(HK)
-    ]
-    stream = state_in + weight_in
+    stream = []
+    for first in range(0, HK, GROUP):
+        heads, rows = pl.ds(2 * first, 2 * GROUP), pl.ds(256 * first, 256 * GROUP)
+        sems = (stream_sem.at[len(stream)], stream_sem.at[len(stream) + 1])
+        stream += [
+            pltpu.make_async_copy(s_hbm.at[:, heads], state_ref.at[:, heads], sems[0]),
+            pltpu.make_async_copy(w_hbm.at[rows], w_in.at[rows], sems[1]),
+        ]
     for copy in small + stream[:AHEAD]:
         copy.start()
     for copy in small:
@@ -134,8 +129,8 @@
     for first in range(0, HK, GROUP):
         group = range(first, first + GROUP)
         span = slice(first * R, (first + GROUP) * R)
+        arrive(2 * first // GROUP)
         for i in group:
-            arrive(i)
             state = jnp.concatenate(
                 [state_ref[:, 2 * i + j].reshape(R * 128, 128).astype(BF16) for j in range(2)],
                 axis=1,
@@ -202,17 +197,17 @@
                         state_ref[r, 2 * i + j] * late[j][3][row : row + 1]
                         + added[:, j * 128 : (j + 1) * 128]
                     )
-    for i in range(HK):
-        arrive(HK + i)
-        part = dot(outs[i], w_in[i * 256 : (i + 1) * 256, :])
-        if i == 0:
-            acc[...] = part
-        elif i < HK - 1:
-            acc[...] += part
-        else:
-            total = acc[...] + part
-            send_ref[...] = total.astype(BF16)
-            own_ref[...] = total + h_in[...].reshape(TOK, D).astype(F32)
+        arrive(2 * first // GROUP + 1)
+        for i in group:
+            part = dot(outs[i], w_in[i * 256 : (i + 1) * 256, :])
+            if i == 0:
+                acc[...] = part
+            elif i < HK - 1:
+                acc[...] += part
+            else:
+                total = acc[...] + part
+                send_ref[...] = total.astype(BF16)
+                own_ref[...] = total + h_in[...].reshape(TOK, D).astype(F32)
 
 
 def core_call(*args):
@@ -236,8 +231,7 @@
             pltpu.VMEM((2 * T, HK * R, 256), F32),
             pltpu.VMEM((TOK, D), F32),
             pltpu.SemaphoreType.DMA((10,)),
-            pltpu.SemaphoreType.DMA((HK,)),
-            pltpu.SemaphoreType.DMA((HK,)),
+            pltpu.SemaphoreType.DMA((2 * HK // GROUP,)),
         ],
         compiler_params=pltpu.CompilerParams(vmem_limit_bytes=CORE_VMEM * MiB),
         cost_estimate=pl.CostEstimate(flops=10**9, bytes_accessed=17 * MiB, transcendentals=10**5),

time: 66.2 us -> 65.6 us (level)
  no operation moved by 1% of the time
where the time goes in v2:
time: 65.6 us; the launch traced here: 65.4 us
  blocking collectives  44.5 us (68%)
  Pallas kernels  14.7 us (22%)
  starting transfers between devices  4.72 us (7%)
  between operations  0.76 us (1%)
    all_to_all x1, blocking collectives, local(): arrived = lax.all_to_all(outbound.reshape(shape), 'ep', 0, 0, tiled=True)  26.5 us
    all_to_all x1, blocking collectives, local(): returned = lax.all_to_all(produced.reshape(shape), 'ep', 0, 0, tiled=True)  18.1 us
    pallas_call x1, Pallas kernels, core_call(): pl.pallas_call(core_kernel, in_specs=[pl.BlockSpec(memory_space=pl.ANY)]...  8.08 us
    ppermute x1, starting transfers between devices, local(): got = lax.ppermute(give, 'hd', swap)  3.21 us
    pallas_call x1, Pallas kernels, expert_call(): pl.pallas_call(expert_kernel, in_specs=[IN_VMEM] * 4 + [AS_IS] * 2, out_s...  2.53 us
    pallas_call x1, Pallas kernels, last_call(): pl.pallas_call(last_kernel, in_specs=[AS_IS] * 2, out_specs=AS_IS, out_sh...  1.68 us
    ppermute x1, starting transfers between devices, local(): got = lax.ppermute(send, 'hd', swap)  1.51 us
    pallas_call x1, Pallas kernels, table_call(): pl.pallas_call(table_kernel, in_specs=[IN_VMEM] * 2 + [AS_IS], out_specs=...  1.34 us
  transfers between devices with their start and end apart: 2, of which 0 were waited for; matrix products, arithmetic and copies ran while one was open for 0% of the time, Pallas kernels for 5%

profile of v2, /device:TPU:1, one launch (start us, length us, event | category | flops | bytes accessed | tf_op | source)
XLA Modules:
  0.0 65.4 jit_solution(5256209642701236304)
XLA Ops:
  0.6 0.0 copy-start.3
  0.6 0.0 copy-start.4
  0.7 8.1 %core.1 = (f32[24,2048]{1,0:T(8,128)S(1)}, bf16[24,2048]{1,0:T(8,128)(2,1)S(1)}, f32[8,16,128,128]{3,2,1,0:T(8,128)S(1)}) custom-call(bf16[8,3,8,128]{3,2,1,0:T(8,128)(2,1)} %q_hbm.1, bf16[8,3,8,128]{3,2,1,0:T(8,128)(2,1)} %k_hbm.1, bf16[8,3,16,128]{3,2,1,0:T(8,128)(2,1)} %v_hbm.1, bf16[8,3,16,128]{3,2,1,0:T(8,128)(2,1)} %g_hbm.1, ...), custom_call_target="tpu_custom_call" | custom-call | flops 1000000000 | bytes 17825792 | tf_op jit(solution)/shard_map/core/pallas_call | solution.py:217
  8.7 0.0 copy-start.5
  8.8 0.0 copy-start
  8.8 0.0 copy-start.1
  8.8 0.0 copy-start.2
  8.8 1.5 %collective-permute-start = (bf16[24,2048]{1,0:T(8,128)(2,1)S(1)}, bf16[24,2048]{1,0:T(8,128)(2,1)S(1)}, u32[]{:S(2)}, u32[]{:S(2)}) collective-permute-start(bf16[24,2048]{1,0:T(8,128)(2,1)S(1)} %get-tuple-element.15), channel_id=1, source_target_pairs={{0,1},{1,0},{2,3},{3,2},{4,5},{5,4},{6,7},{7,6},{8,9},{9,8},{10,11... | collective-permute-start | bytes 294920 | tf_op jit(solution)/shard_map/ppermute | solution.py:484
  10.3 0.0 copy-done.3
  10.3 0.0 copy-done.4
  10.3 1.3 %tables.1 = (bf16[3,512,256]{2,1,0:T(8,128)(2,1)S(1)}, bf16[3,64,512]{2,1,0:T(8,128)(2,1)S(1)}, f32[8,16,128,128]{3,2,1,0:T(8,128)}) custom-call(s32[3,8,10]{2,1,0:T(8,128)S(1)} %bitcast.21, f32[3,8,10]{2,1,0:T(8,128)S(1)} %bitcast.22, f32[8,16,128,128]{3,2,1,0:T(8,128)S(1)} %get-tuple-element.16.state_ref), custom_call_target="tpu_custom_call" | custom-call | flops 100000000 | bytes 1000000 | tf_op jit(solution)/shard_map/tables/pallas_call | solution.py:292
  11.7 0.0 collective-permute-done.got_ref
  11.7 0.0 copy-done.5
  11.7 0.5 dispatch.1
  12.2 26.5 %all_to_all.10 = bf16[64,8,768]{2,1,0:T(8,128)(2,1)S(1)} all-to-all(bf16[64,8,768]{2,1,0:T(8,128)(2,1)S(1)} %bitcast.19), channel_id=1, replica_groups=mesh['ep'=64,'hd'=2] {'ep'}, dimensions={0} | all-to-all | bytes 1572864 | tf_op jit(solution)/shard_map/all_to_all | solution.py:488
  38.6 0.0 copy-done
  38.6 0.0 copy-done.2
  38.6 2.5 %expert.1 = (bf16[512,768]{1,0:T(8,128)(2,1)S(1)}, f32[8,16,128,128]{3,2,1,0:T(8,128)}) custom-call(bf16[512,768]{1,0:T(8,128)(2,1)S(1)} %bitcast.17, bf16[1,2048,512]{2,1,0:T(8,128)(2,1)S(1)} %copy-done, bf16[1,2048,512]{2,1,0:T(8,128)(2,1)S(1)} %copy-done.1, bf16[1,512,2048]{2,1,0:T(8,128)(2,1)S(1)} %copy-done.2, ...), custom_call_target="tpu_custom_call", output_to_operand_aliasing={{1}: (5, {})} | custom-call | flops 1200000000 | bytes 8000000 | tf_op jit(solution)/shard_map/expert/pallas_call | solution.py:364
  41.2 18.1 %all_to_all.11 = bf16[64,8,768]{2,1,0:T(8,128)(2,1)S(1)} all-to-all(bf16[64,8,768]{2,1,0:T(8,128)(2,1)S(1)} %bitcast.20), channel_id=1, replica_groups=mesh['ep'=64,'hd'=2] {'ep'}, dimensions={0} | all-to-all | bytes 1572864 | tf_op jit(solution)/shard_map/all_to_all | solution.py:492
  59.2 0.6 combine.1
  59.8 3.2 %collective-permute-start.1 = (bf16[24,1024]{1,0:T(8,128)(2,1)S(1)}, bf16[24,1024]{1,0:T(8,128)(2,1)S(1)}, u32[]{:S(2)}, u32[]{:S(2)}) collective-permute-start(bf16[24,1024]{1,0:T(8,128)(2,1)S(1)} %get-tuple-element.24), channel_id=1, source_target_pairs={{0,1},{1,0},{2,3},{3,2},{4,5},{5,4},{6,7},{7,6},{8,9},{9,8},{10,11... | collective-permute-start | bytes 147464 | tf_op jit(solution)/shard_map/ppermute | solution.py:494
  63.1 1.7 %last.1 = f32[8,16,128,128]{3,2,1,0:T(8,128)} custom-call(f32[8,16,128,128]{3,2,1,0:T(8,128)S(1)} %get-tuple-element.16.state_ref, f32[8,16,128,128]{3,2,1,0:T(8,128)} %get-tuple-element.25.held_ref), custom_call_target="tpu_custom_call", output_to_operand_aliasing={{}: (1, {})} | custom-call | bytes 6291456 | tf_op jit(solution)/shard_map/last/pallas_call | solution.py:430
  64.7 0.0 collective-permute-done.1
  64.8 0.6 fusion
  (1 shorter events, 0.0 us)
Async XLA Ops:
  0.6 9.7 %copy-start.3 = (s32[8,3,10]{2,0,1:T(8,128)S(1)}, s32[8,3,10]{2,0,1:T(8,128)}, u32[]{:S(2)}) copy-start(s32[8,3,10]{2,0,1:T(8,128)} %param.30) | copy-start | bytes 2884
  0.6 9.7 %copy-start.4 = (f32[8,3,10]{2,0,1:T(8,128)S(1)}, f32[8,3,10]{2,0,1:T(8,128)}, u32[]{:S(2)}) copy-start(f32[8,3,10]{2,0,1:T(8,128)} %param.31) | copy-start | bytes 2884
  8.7 2.9 %copy-start.5 = (f32[2048]{0:T(1024)S(1)}, f32[2048]{0:T(1024)}, u32[]{:S(2)}) copy-start(f32[2048]{0:T(1024)} %param.29) | copy-start | bytes 24580
  8.8 29.9 %copy-start = (bf16[1,2048,512]{2,1,0:T(8,128)(2,1)S(1)}, bf16[1,2048,512]{2,1,0:T(8,128)(2,1)}, u32[]{:S(2)}) copy-start(bf16[1,2048,512]{2,1,0:T(8,128)(2,1)} %gate_ref.1) | copy-start | bytes 6291460
  8.8 29.9 %copy-start.1 = (bf16[1,2048,512]{2,1,0:T(8,128)(2,1)S(1)}, bf16[1,2048,512]{2,1,0:T(8,128)(2,1)}, u32[]{:S(2)}) copy-start(bf16[1,2048,512]{2,1,0:T(8,128)(2,1)} %up_ref.1) | copy-start | bytes 6291460
  8.8 29.9 %copy-start.2 = (bf16[1,512,2048]{2,1,0:T(8,128)(2,1)S(1)}, bf16[1,512,2048]{2,1,0:T(8,128)(2,1)}, u32[]{:S(2)}) copy-start(bf16[1,512,2048]{2,1,0:T(8,128)(2,1)} %down_ref.1) | copy-start | bytes 6291460
  8.8 2.9 %collective-permute-start = (bf16[24,2048]{1,0:T(8,128)(2,1)S(1)}, bf16[24,2048]{1,0:T(8,128)(2,1)S(1)}, u32[]{:S(2)}, u32[]{:S(2)}) collective-permute-start(bf16[24,2048]{1,0:T(8,128)(2,1)S(1)} %get-tuple-element.15), channel_id=1, source_target_pairs={{0,1},{1,0},{2,3},{3,2},{4,5},{5,4},{6,7},{7,6},{8,9},{9,8},{10,11... | collective-permute-start | bytes 294920 | tf_op jit(solution)/shard_map/ppermute | solution.py:484
  59.8 4.9 %collective-permute-start.1 = (bf16[24,1024]{1,0:T(8,128)(2,1)S(1)}, bf16[24,1024]{1,0:T(8,128)(2,1)S(1)}, u32[]{:S(2)}, u32[]{:S(2)}) collective-permute-start(bf16[24,1024]{1,0:T(8,128)(2,1)S(1)} %get-tuple-element.24), channel_id=1, source_target_pairs={{0,1},{1,0},{2,3},{3,2},{4,5},{5,4},{6,7},{7,6},{8,9},{9,8},{10,11... | collective-permute-start | bytes 147464 | tf_op jit(solution)/shard_map/ppermute | solution.py:494

commit v3 on v2

--- a/solution.py
+++ b/solution.py
@@ -21,12 +21,9 @@
 PC = D // PARTS
 TP = 32
 MiB = 1 << 20
-CORE_VMEM = 55
-GROUP = 2
-AHEAD = 3
-FLUSH_FIRST = (0, 1)
-FLUSH_NEXT = (2, 3, 4)
-FLUSH_LAST = (5, 6, 7)
+CORE_VMEM = 62
+GROUP = 4
+AHEAD = 2
 
 
 def dot(a, b, dims=((1,), (0,))):
@@ -39,9 +36,9 @@
 
 def core_kernel(
     q_hbm, k_hbm, v_hbm, g_hbm, a_hbm, b_hbm, scale_hbm, bias_hbm, gain_hbm, h_hbm, s_hbm, w_hbm,
-    own_ref, send_ref, state_ref,
-    q_in, k_in, v_in, g_in, a_in, b_in, scale_in, bias_in, gain_in, h_in, w_in,
-    qs, ks, vs, gs, fs, bs, lhs, seen, acc, small_sem, stream_sem,
+    own_ref, send_ref, k_hbm_out, u_hbm_out, f_hbm_out,
+    q_in, k_in, v_in, g_in, a_in, b_in, scale_in, bias_in, gain_in, h_in, w_in, state_ref, ku_ref, uu_ref, f3_ref,
+    qs, ks, vs, gs, fs, bs, lhs, seen, acc, small_sem, stream_sem, out_sem,
 ):
     small = [
         pltpu.make_async_copy(source, target, small_sem.at[i])
@@ -119,13 +116,9 @@
     kk21, kk31, kk32 = pair(kt[1], kt[0]), pair(kt[2], kt[0]), pair(kt[2], kt[1])
     qk = [[pair(qt[t], kt[s]) for s in range(t + 1)] for t in range(T)]
 
-    def split(x):
-        high = x.astype(BF16).astype(F32)
-        return high, x - high
-
     gain = gain_in[...]
-    lane_of = iota((128, 3 * TOK), 1) % R
     outs = []
+    written = []
     for first in range(0, HK, GROUP):
         group = range(first, first + GROUP)
         span = slice(first * R, (first + GROUP) * R)
@@ -180,23 +173,19 @@
                     [jnp.concatenate([x[at] for x in done[j]], axis=0) for j in range(2)], axis=1
                 ).astype(BF16)
             )
-            key_high, key_low = split(
-                jnp.concatenate([x[i * R : (i + 1) * R] for x in kt], axis=0)
+            ku_ref[i] = jnp.concatenate([x[i * R : (i + 1) * R] for x in kt], axis=0)
+            for j in range(2):
+                lanes = slice(j * 128, (j + 1) * 128)
+                uu_ref[i, :, lanes] = jnp.concatenate([x[at] for x in late[j][:3]], axis=0)
+                f3_ref[i, :, lanes] = late[j][3][at]
+        for source, target in ((ku_ref, k_hbm_out), (uu_ref, u_hbm_out), (f3_ref, f_hbm_out)):
+            span = pl.ds(first, GROUP)
+            written.append(
+                pltpu.make_async_copy(
+                    source.at[span], target.at[span], out_sem.at[len(written)]
+                )
             )
-            keys = jnp.concatenate([key_high, key_low, key_high], axis=0).T
-            update = jnp.concatenate(
-                [jnp.concatenate([x[at] for x in late[j][:3]], axis=0) for j in range(2)], axis=1
-            )
-            up_high, up_low = split(update)
-            update = jnp.concatenate([up_high, up_high, up_low], axis=0).astype(BF16)
-            for r in range(R):
-                added = dot(jnp.where(lane_of == r, keys, 0.0).astype(BF16), update)
-                row = (i - first) * R + r
-                for j in range(2):
-                    state_ref[r, 2 * i + j] = (
-                        state_ref[r, 2 * i + j] * late[j][3][row : row + 1]
-                        + added[:, j * 128 : (j + 1) * 128]
-                    )
+            written[-1].start()
         arrive(2 * first // GROUP + 1)
         for i in group:
             part = dot(outs[i], w_in[i * 256 : (i + 1) * 256, :])
@@ -208,6 +197,8 @@
                 total = acc[...] + part
                 send_ref[...] = total.astype(BF16)
                 own_ref[...] = total + h_in[...].reshape(TOK, D).astype(F32)
+    for copy in written:
+        copy.wait()
 
 
 def core_call(*args):
@@ -217,13 +208,18 @@
     return pl.pallas_call(
         core_kernel,
         in_specs=[pl.BlockSpec(memory_space=pl.ANY)] * len(args),
-        out_specs=[pl.BlockSpec(memory_space=pltpu.VMEM)] * 3,
+        out_specs=[pl.BlockSpec(memory_space=pltpu.VMEM)] * 2
+        + [pl.BlockSpec(memory_space=pl.ANY)] * 3,
         out_shape=[
             pltpu.VMEM((TOK, D), F32),
             pltpu.VMEM((TOK, D), BF16),
-            pltpu.VMEM(state.shape, F32),
+            pltpu.HBM((HK, TOK, 128), F32),
+            pltpu.HBM((HK, TOK, 256), F32),
+            pltpu.HBM((HK, R, 256), F32),
         ],
         scratch_shapes=landing
+        + [pltpu.VMEM(state.shape, F32)]
+        + [pltpu.VMEM((HK, rows, width), F32) for rows, width in ((TOK, 128), (TOK, 256), (R, 256))]
         + [pltpu.VMEM((HK * TOK, 128), F32)] * 2
         + [pltpu.VMEM((2 * HK * TOK, 128), F32)] * 4
         + [
@@ -232,6 +228,7 @@
             pltpu.VMEM((TOK, D), F32),
             pltpu.SemaphoreType.DMA((10,)),
             pltpu.SemaphoreType.DMA((2 * HK // GROUP,)),
+            pltpu.SemaphoreType.DMA((3 * HK // GROUP,)),
         ],
         compiler_params=pltpu.CompilerParams(vmem_limit_bytes=CORE_VMEM * MiB),
         cost_estimate=pl.CostEstimate(flops=10**9, bytes_accessed=17 * MiB, transcendentals=10**5),
@@ -239,18 +236,70 @@
     )(*args)
 
 
-def flush(state_ref, out_ref, sem, chunks):
-    copies = []
-    for n, i in enumerate(chunks):
-        part = pl.ds(2 * i, 2)
-        copies.append(pltpu.make_async_copy(state_ref.at[:, part], out_ref.at[:, part], sem.at[n]))
-    for copy in copies:
+def state_kernel(
+    s_hbm, k_hbm, u_hbm, f_hbm, after_ref, o_hbm,
+    state, k_in, u_in, f_in, small_sem, in_sem, out_sem,
+):
+    small = [
+        pltpu.make_async_copy(source, target, small_sem.at[n])
+        for n, (source, target) in enumerate(((k_hbm, k_in), (u_hbm, u_in), (f_hbm, f_in)))
+    ]
+    reads, writes = [], []
+    for i in range(HK):
+        heads = pl.ds(2 * i, 2)
+        reads.append(pltpu.make_async_copy(s_hbm.at[:, heads], state.at[:, heads], in_sem.at[i]))
+        writes.append(pltpu.make_async_copy(state.at[:, heads], o_hbm.at[:, heads], out_sem.at[i]))
+    for copy in small + reads:
         copy.start()
-    return copies
-
-
-def table_kernel(ids_ref, route_ref, state_ref, pick_ref, mix_ref, out_ref, sem):
-    copies = flush(state_ref, out_ref, sem, FLUSH_FIRST)
+    for copy in small:
+        copy.wait()
+
+    def split(x):
+        high = x.astype(BF16).astype(F32)
+        return high, x - high
+
+    row_of = iota((128, 3 * TOK), 1) % R
+    for i in range(HK):
+        k_high, k_low = split(k_in[i])
+        u_high, u_low = split(u_in[i])
+        keys = jnp.concatenate([k_high, k_low, k_high], axis=0).T
+        updates = jnp.concatenate([u_high, u_high, u_low], axis=0).astype(BF16)
+        reads[i].wait()
+        for r in range(R):
+            own = jnp.where(row_of == r, keys, 0.0).astype(BF16)
+            added = dot(own, updates)
+            for j in range(2):
+                lanes = slice(j * 128, (j + 1) * 128)
+                state[r, 2 * i + j] = (
+                    state[r, 2 * i + j] * f_in[i, r : r + 1, lanes] + added[:, lanes]
+                )
+        writes[i].start()
+    for copy in writes:
+        copy.wait()
+
+
+def state_call(state, keys, updates, factor, after):
+    args = [
+        pltpu.with_memory_space_constraint(x, pltpu.HBM) for x in (state, keys, updates, factor)
+    ]
+    return pl.pallas_call(
+        state_kernel,
+        in_specs=[pl.BlockSpec(memory_space=pl.ANY)] * 5,
+        out_specs=pl.BlockSpec(memory_space=pl.ANY),
+        out_shape=pltpu.HBM(state.shape, F32),
+        scratch_shapes=[pltpu.VMEM(x.shape, F32) for x in args]
+        + [
+            pltpu.SemaphoreType.DMA((3,)),
+            pltpu.SemaphoreType.DMA((HK,)),
+            pltpu.SemaphoreType.DMA((HK,)),
+        ],
+        compiler_params=pltpu.CompilerParams(vmem_limit_bytes=16 * MiB),
+        cost_estimate=pl.CostEstimate(flops=10**9, bytes_accessed=17 * MiB, transcendentals=0),
+        name="state",
+    )(*args, pltpu.with_memory_space_constraint(after, pltpu.HBM))
+
+
+def table_kernel(ids_ref, route_ref, state_ref, pick_ref, mix_ref):
     parity = lax.axis_index("hd")
     ids = ids_ref[...].reshape(TOK, -1)
     route = route_ref[...].reshape(TOK, -1)
@@ -280,29 +329,20 @@
         high = share.astype(BF16).astype(F32)
         parts = jnp.concatenate([high, share - high], axis=0).astype(BF16)
         mix_ref[s] = dot(parts, across).astype(BF16)
-    for copy in copies:
-        copy.wait()
-
-
-IN_VMEM = pl.BlockSpec(memory_space=pltpu.VMEM)
-AS_IS = pl.BlockSpec(memory_space=pl.ANY)
 
 
 def table_call(ids, route, state):
     return pl.pallas_call(
         table_kernel,
-        in_specs=[IN_VMEM] * 2 + [AS_IS],
-        out_specs=[IN_VMEM] * 2 + [AS_IS],
+        in_specs=[pl.BlockSpec(memory_space=pltpu.VMEM)] * 2 + [pl.BlockSpec(memory_space=pl.ANY)],
         out_shape=[
             jax.ShapeDtypeStruct((SLOTS, CHIPS * PARTS, PARTS * TP), BF16),
             jax.ShapeDtypeStruct((SLOTS, 2 * TP, CHIPS * PARTS), BF16),
-            pltpu.HBM(state.shape, F32),
-        ],
-        scratch_shapes=[pltpu.SemaphoreType.DMA((len(FLUSH_FIRST),))],
+        ],
         compiler_params=pltpu.CompilerParams(vmem_limit_bytes=16 * MiB),
         cost_estimate=pl.CostEstimate(flops=10**8, bytes_accessed=10**6, transcendentals=0),
         name="tables",
-    )(ids, route, pltpu.with_memory_space_constraint(state, pltpu.VMEM))
+    )(ids, route, pltpu.with_memory_space_constraint(state, pltpu.HBM))
 
 
 def dispatch_kernel(own_ref, got_ref, gain_ref, pick_ref, res_ref, out_ref):
@@ -332,10 +372,7 @@
     )(own, got, gain, pick)
 
 
-def expert_kernel(
-    x_ref, gate_ref, up_ref, down_ref, state_ref, held_ref, y_ref, out_ref, wide, sem
-):
-    copies = flush(state_ref, out_ref, sem, FLUSH_NEXT)
+def expert_kernel(x_ref, gate_ref, up_ref, down_ref, y_hbm, wide, y_out, sem):
     chunks = SLOTS * PC // 128
     for c in range(chunks):
         wide[c] = x_ref[:, c * 128 : (c + 1) * 128].astype(F32)
@@ -354,39 +391,36 @@
         for c in range(chunks):
             at, side = c // 2 * CHIPS, c % 2 * 128
             wide[c, pl.ds(p, CHIPS, stride=PARTS), :] = y[at : at + CHIPS, side : side + 128]
+    copies = []
     for c in range(chunks):
-        y_ref[:, c * 128 : (c + 1) * 128] = wide[c].astype(BF16)
+        lanes = slice(c * 128, (c + 1) * 128)
+        y_out[:, lanes] = wide[c].astype(BF16)
+        lanes = pl.ds(c * 128, 128)
+        copies.append(pltpu.make_async_copy(y_out.at[:, lanes], y_hbm.at[:, lanes], sem.at[c]))
+        copies[c].start()
     for copy in copies:
         copy.wait()
 
 
-def expert_call(x, gate, up, down, state, held):
+def expert_call(x, gate, up, down):
     return pl.pallas_call(
         expert_kernel,
-        in_specs=[IN_VMEM] * 4 + [AS_IS] * 2,
-        out_specs=[IN_VMEM, AS_IS],
-        out_shape=[jax.ShapeDtypeStruct(x.shape, BF16), pltpu.HBM(state.shape, F32)],
-        input_output_aliases={5: 1},
+        out_specs=pl.BlockSpec(memory_space=pl.ANY),
+        out_shape=pltpu.HBM(x.shape, BF16),
         scratch_shapes=[
             pltpu.VMEM((x.shape[1] // 128, x.shape[0], 128), F32),
-            pltpu.SemaphoreType.DMA((len(FLUSH_NEXT),)),
+            pltpu.VMEM(x.shape, BF16),
+            pltpu.SemaphoreType.DMA((x.shape[1] // 128,)),
         ],
         compiler_params=pltpu.CompilerParams(vmem_limit_bytes=24 * MiB),
         cost_estimate=pl.CostEstimate(
             flops=12 * 10**8, bytes_accessed=8 * 10**6, transcendentals=10**5
         ),
         name="expert",
-    )(
-        x,
-        gate,
-        up,
-        down,
-        pltpu.with_memory_space_constraint(state, pltpu.VMEM),
-        pltpu.with_memory_space_constraint(held, pltpu.HBM),
-    )
-
-
-def combine_kernel(y_ref, mix_ref, res_ref, keep_ref, send_ref):
+    )(x, gate, up, down)
+
+
+def combine_kernel(y_ref, mix_ref, res_ref, state_ref, keep_ref, send_ref, out_ref):
     parity = lax.axis_index("hd")
     part_of = iota((2 * TP, CHIPS * PARTS), 1) % PARTS
     half = D // 2
@@ -408,39 +442,23 @@
     send_ref[...] = jnp.where(first, high, low).astype(BF16)
 
 
-def combine_call(y, mix, residual):
+def combine_call(y, mix, residual, state):
+    vmem = pl.BlockSpec(memory_space=pltpu.VMEM)
+    held = pl.BlockSpec(memory_space=pl.ANY)
     return pl.pallas_call(
         combine_kernel,
+        in_specs=[vmem, vmem, vmem, held],
+        out_specs=[vmem, vmem, held],
         out_shape=[
             jax.ShapeDtypeStruct((TOK, D // 2), F32),
             jax.ShapeDtypeStruct((TOK, D // 2), BF16),
-        ],
+            pltpu.HBM(state.shape, F32),
+        ],
+        input_output_aliases={3: 2},
         compiler_params=pltpu.CompilerParams(vmem_limit_bytes=24 * MiB),
         cost_estimate=pl.CostEstimate(flops=4 * 10**8, bytes_accessed=10**6, transcendentals=0),
         name="combine",
-    )(y, mix, residual)
-
-
-def last_kernel(state_ref, held_ref, out_ref, sem):
-    for copy in flush(state_ref, out_ref, sem, FLUSH_LAST):
-        copy.wait()
-
-
-def last_call(state, held):
-    return pl.pallas_call(
-        last_kernel,
-        in_specs=[AS_IS] * 2,
-        out_specs=AS_IS,
-        out_shape=pltpu.HBM(state.shape, F32),
-        input_output_aliases={1: 0},
-        scratch_shapes=[pltpu.SemaphoreType.DMA((len(FLUSH_LAST),))],
-        compiler_params=pltpu.CompilerParams(vmem_limit_bytes=4 * MiB),
-        cost_estimate=pl.CostEstimate(flops=0, bytes_accessed=6 * MiB, transcendentals=0),
-        name="last",
-    )(
-        pltpu.with_memory_space_constraint(state, pltpu.VMEM),
-        pltpu.with_memory_space_constraint(held, pltpu.HBM),
-    )
+    )(y, mix, residual, pltpu.with_memory_space_constraint(state, pltpu.HBM))
 
 
 def local(
@@ -466,7 +484,7 @@
     def by_step(x):
         return jnp.transpose(x, (1, 0, 2))
 
-    own, send, fresh = core_call(
+    own, send, keys, updates, factor = core_call(
         new_queries,
         new_keys,
         new_values,
@@ -482,17 +500,17 @@
     )
     swap = [(0, 1), (1, 0)]
     got = lax.ppermute(send, "hd", swap)
-    pick, mix, held = table_call(by_step(expert_ids), by_step(route_weight), fresh)
+    pick, mix = table_call(by_step(expert_ids), by_step(route_weight), old_state)
     residual, outbound = dispatch_call(own, got, norm_gain.reshape(1, -1), pick)
     shape = (CHIPS, PARTS, SLOTS * PC)
     arrived = lax.all_to_all(outbound.reshape(shape), "ep", 0, 0, tiled=True)
-    produced, held = expert_call(
-        arrived.reshape(outbound.shape), gate_weight, up_weight, down_weight, fresh, held
+    produced = expert_call(arrived.reshape(outbound.shape), gate_weight, up_weight, down_weight)
+    new_state = state_call(old_state, keys, updates, factor, produced)
+    returned = lax.all_to_all(produced.reshape(shape), "ep", 0, 0, tiled=True)
+    keep, give, new_state = combine_call(
+        returned.reshape(outbound.shape), mix, residual, new_state
     )
-    returned = lax.all_to_all(produced.reshape(shape), "ep", 0, 0, tiled=True)
-    keep, give = combine_call(returned.reshape(outbound.shape), mix, residual)
     got = lax.ppermute(give, "hd", swap)
-    new_state = last_call(fresh, held)
     total = keep + got.astype(F32)
     output_rows = by_step(total.astype(BF16).reshape(T, R, -1))
     return (output_rows, new_state)

time: 65.6 us -> 64.3 us (0.980)
  blocking collectives: 44.5 us -> 26.2 us
  waiting for transfers between devices: 0.01 us -> 7.94 us
  starting transfers between devices: 4.72 us -> 9.31 us
  Pallas kernels: 14.7 us -> 19.1 us
    all_to_all x1 -> x0, blocking collectives: 18.1 us -> none  [local(): returned = lax.all_to_all(produced.reshape(shape), 'ep', 0, 0, tiled=True)]
    all_to_all x0 -> x1, waiting for transfers between devices: none -> 7.05 us  [local(): returned = lax.all_to_all(produced.reshape(shape), 'ep', 0, 0, tiled=True)]
    pallas_call x4, Pallas kernels: 6.16 us -> 11.1 us  [the longest x1 6.94 us: state_call(): pl.pallas_call(state_kernel, in_specs=[pl.BlockSpec(memory_space=pl.ANY)]...]
    all_to_all x0 -> x1, starting transfers between devices: none -> 4.65 us  [local(): returned = lax.all_to_all(produced.reshape(shape), 'ep', 0, 0, tiled=True)]
    ppermute x1, waiting for transfers between devices: 0.01 us -> 0.88 us  [local(): got = lax.ppermute(give, 'hd', swap)]
  transfers between devices with their start and end apart: 2 -> 3, of which waited for: 0 -> 2; matrix products, arithmetic and copies ran while one was open for 0% -> 0% of each run, Pallas kernels for 5% -> 12%
where the time goes in v3:
time: 64.3 us; the launch traced here: 64.1 us
  blocking collectives  26.2 us (41%)
  Pallas kernels  19.1 us (30%)
  starting transfers between devices  9.31 us (14%)
  waiting for transfers between devices  7.94 us (12%)
  between operations  0.76 us (1%)
    all_to_all x1, blocking collectives, local(): arrived = lax.all_to_all(outbound.reshape(shape), 'ep', 0, 0, tiled=True)  26.2 us
    pallas_call x1, Pallas kernels, core_call(): pl.pallas_call(core_kernel, in_specs=[pl.BlockSpec(memory_space=pl.ANY)]...  7.55 us
    all_to_all x1, waiting for transfers between devices, local(): returned = lax.all_to_all(produced.reshape(shape), 'ep', 0, 0, tiled=True)  7.05 us
    pallas_call x1, Pallas kernels, state_call(): pl.pallas_call(state_kernel, in_specs=[pl.BlockSpec(memory_space=pl.ANY)]...  6.94 us
    all_to_all x1, starting transfers between devices, local(): returned = lax.all_to_all(produced.reshape(shape), 'ep', 0, 0, tiled=True)  4.65 us
    ppermute x1, starting transfers between devices, local(): got = lax.ppermute(give, 'hd', swap)  3.16 us
    pallas_call x1, Pallas kernels, expert_call(): pl.pallas_call(expert_kernel, out_specs=pl.BlockSpec(memory_space=pl.ANY)...  2.59 us
    ppermute x1, starting transfers between devices, local(): got = lax.ppermute(send, 'hd', swap)  1.5 us
  transfers between devices with their start and end apart: 3, of which 2 were waited for; matrix products, arithmetic and copies ran while one was open for 0% of the time, Pallas kernels for 12%

profile of v3, /device:TPU:1, one launch (start us, length us, event | category | flops | bytes accessed | tf_op | source)
XLA Modules:
  0.0 64.1 jit_solution(16512183462293351413)
XLA Ops:
  0.6 0.0 copy-start.3
  0.6 0.0 copy-start.4
  0.7 7.6 %core.1 = (f32[24,2048]{1,0:T(8,128)S(1)}, bf16[24,2048]{1,0:T(8,128)(2,1)S(1)}, f32[8,24,128]{2,1,0:T(8,128)}, f32[8,24,256]{2,1,0:T(8,128)}, f32[8,8,256]{2,1,0:T(8,128)}) custom-call(bf16[8,3,8,128]{3,2,1,0:T(8,128)(2,1)} %q_hbm.1, bf16[8,3,8,128]{3,2,1,0:T(8,128)(2,1)} %k_hbm.1, bf16[8,3,16,128]{3,2,1,0:T(8,128)(2,1)} %v_hbm.1, ...), custom_call_target="tpu_custom_call" | custom-call | flops 1000000000 | bytes 17825792 | tf_op jit(solution)/shard_map/core/pallas_call | solution.py:208
  8.2 0.0 copy-start.5
  8.2 0.0 copy-start
  8.2 0.0 copy-start.1
  8.3 0.0 copy-start.2
  8.3 1.5 %collective-permute-start = (bf16[24,2048]{1,0:T(8,128)(2,1)S(1)}, bf16[24,2048]{1,0:T(8,128)(2,1)S(1)}, u32[]{:S(2)}, u32[]{:S(2)}) collective-permute-start(bf16[24,2048]{1,0:T(8,128)(2,1)S(1)} %get-tuple-element.15), channel_id=1, source_target_pairs={{0,1},{1,0},{2,3},{3,2},{4,5},{5,4},{6,7},{7,6},{8,9},{9,8},{10,11... | collective-permute-start | bytes 294920 | tf_op jit(solution)/shard_map/ppermute | solution.py:502
  9.8 0.0 copy-done.3
  9.8 0.0 copy-done.4
  9.8 0.9 %tables.1 = (bf16[3,512,256]{2,1,0:T(8,128)(2,1)S(1)}, bf16[3,64,512]{2,1,0:T(8,128)(2,1)S(1)}) custom-call(s32[3,8,10]{2,1,0:T(8,128)S(1)} %bitcast.20, f32[3,8,10]{2,1,0:T(8,128)S(1)} %bitcast.21, f32[8,16,128,128]{3,2,1,0:T(8,128)} %s_hbm.3), custom_call_target="tpu_custom_call" | custom-call | flops 100000000 | bytes 1000000 | tf_op jit(solution)/shard_map/tables/pallas_call | solution.py:335
  10.7 0.0 collective-permute-done.got_ref
  10.7 0.0 copy-done.5
  10.7 0.5 dispatch.1
  11.2 26.2 %all_to_all.10 = bf16[64,8,768]{2,1,0:T(8,128)(2,1)S(1)} all-to-all(bf16[64,8,768]{2,1,0:T(8,128)(2,1)S(1)} %bitcast.19), channel_id=1, replica_groups=mesh['ep'=64,'hd'=2] {'ep'}, dimensions={0} | all-to-all | bytes 1572864 | tf_op jit(solution)/shard_map/all_to_all | solution.py:506
  37.5 0.0 copy-done.1
  37.5 2.6 %expert.1.after_ref = bf16[512,768]{1,0:T(8,128)(2,1)} custom-call(bf16[512,768]{1,0:T(8,128)(2,1)S(1)} %bitcast.18, bf16[1,2048,512]{2,1,0:T(8,128)(2,1)S(1)} %copy-done, bf16[1,2048,512]{2,1,0:T(8,128)(2,1)S(1)} %copy-done.1, bf16[1,512,2048]{2,1,0:T(8,128)(2,1)S(1)} %copy-done.2), custom_call_target="tpu_custom_call" | custom-call | flops 1200000000 | bytes 8000000 | tf_op jit(solution)/shard_map/expert/pallas_call | solution.py:406
  40.1 4.7 %all-to-all-start.1 = ((bf16[64,8,768]{2,1,0:T(8,128)(2,1)}), bf16[64,8,768]{2,1,0:T(8,128)(2,1)S(1)}, u32[]{:S(2)}, u32[]{:S(2)}) async-start(bf16[64,8,768]{2,1,0:T(8,128)(2,1)} %bitcast.23), calls=%async_computation.1 | async-start | bytes 1572864 | tf_op jit(solution)/shard_map/all_to_all | solution.py:509
  44.8 6.9 %state.1.state_ref = f32[8,16,128,128]{3,2,1,0:T(8,128)} custom-call(f32[8,16,128,128]{3,2,1,0:T(8,128)} %s_hbm.3, f32[8,24,128]{2,1,0:T(8,128)} %get-tuple-element.20.k_hbm, f32[8,24,256]{2,1,0:T(8,128)} %get-tuple-element.21.u_hbm, f32[8,8,256]{2,1,0:T(8,128)} %get-tuple-element.22.f_hbm, bf16[512,768]{1,0:T(8,128)(2,1)} %expert.1.after_ref), custom_call_target="tpu_custom_call" | custom-call | flops 1000000000 | bytes 17825792 | tf_op jit(solution)/shard_map/state/pallas_call | solution.py:285
  51.7 7.1 %all-to-all-done.1 = bf16[64,8,768]{2,1,0:T(8,128)(2,1)S(1)} async-done(((bf16[64,8,768]{2,1,0:T(8,128)(2,1)}), bf16[64,8,768]{2,1,0:T(8,128)(2,1)S(1)}, u32[]{:S(2)}, u32[]{:S(2)}) %all-to-all-start.1) | async-done | bytes 786464 | tf_op jit(solution)/shard_map/all_to_all | solution.py:509
  58.8 0.6 combine.1
  59.4 3.2 %collective-permute-start.1 = (bf16[24,1024]{1,0:T(8,128)(2,1)S(1)}, bf16[24,1024]{1,0:T(8,128)(2,1)S(1)}, u32[]{:S(2)}, u32[]{:S(2)}) collective-permute-start(bf16[24,1024]{1,0:T(8,128)(2,1)S(1)} %get-tuple-element.24), channel_id=1, source_target_pairs={{0,1},{1,0},{2,3},{3,2},{4,5},{5,4},{6,7},{7,6},{8,9},{9,8},{10,11... | collective-permute-start | bytes 147464 | tf_op jit(solution)/shard_map/ppermute | solution.py:513
  62.5 0.9 %collective-permute-done.1 = bf16[24,1024]{1,0:T(8,128)(2,1)S(1)} collective-permute-done((bf16[24,1024]{1,0:T(8,128)(2,1)S(1)}, bf16[24,1024]{1,0:T(8,128)(2,1)S(1)}, u32[]{:S(2)}, u32[]{:S(2)}) %collective-permute-start.1) | collective-permute-done | bytes 49184 | tf_op jit(solution)/shard_map/ppermute | solution.py:513
  63.4 0.6 fusion
  (2 shorter events, 0.0 us)
Async XLA Ops:
  0.6 9.1 %copy-start.3 = (s32[8,3,10]{2,0,1:T(8,128)S(1)}, s32[8,3,10]{2,0,1:T(8,128)}, u32[]{:S(2)}) copy-start(s32[8,3,10]{2,0,1:T(8,128)} %param.30) | copy-start | bytes 2884
  0.6 9.1 %copy-start.4 = (f32[8,3,10]{2,0,1:T(8,128)S(1)}, f32[8,3,10]{2,0,1:T(8,128)}, u32[]{:S(2)}) copy-start(f32[8,3,10]{2,0,1:T(8,128)} %param.31) | copy-start | bytes 2884
  8.2 2.5 %copy-start.5 = (f32[2048]{0:T(1024)S(1)}, f32[2048]{0:T(1024)}, u32[]{:S(2)}) copy-start(f32[2048]{0:T(1024)} %param.29) | copy-start | bytes 24580
  8.2 29.3 %copy-start = (bf16[1,2048,512]{2,1,0:T(8,128)(2,1)S(1)}, bf16[1,2048,512]{2,1,0:T(8,128)(2,1)}, u32[]{:S(2)}) copy-start(bf16[1,2048,512]{2,1,0:T(8,128)(2,1)} %gate_ref.1) | copy-start | bytes 6291460
  8.2 29.3 %copy-start.1 = (bf16[1,2048,512]{2,1,0:T(8,128)(2,1)S(1)}, bf16[1,2048,512]{2,1,0:T(8,128)(2,1)}, u32[]{:S(2)}) copy-start(bf16[1,2048,512]{2,1,0:T(8,128)(2,1)} %up_ref.1) | copy-start | bytes 6291460
  8.3 29.2 %copy-start.2 = (bf16[1,512,2048]{2,1,0:T(8,128)(2,1)S(1)}, bf16[1,512,2048]{2,1,0:T(8,128)(2,1)}, u32[]{:S(2)}) copy-start(bf16[1,512,2048]{2,1,0:T(8,128)(2,1)} %down_ref.1) | copy-start | bytes 6291460
  8.3 2.5 %collective-permute-start = (bf16[24,2048]{1,0:T(8,128)(2,1)S(1)}, bf16[24,2048]{1,0:T(8,128)(2,1)S(1)}, u32[]{:S(2)}, u32[]{:S(2)}) collective-permute-start(bf16[24,2048]{1,0:T(8,128)(2,1)S(1)} %get-tuple-element.15), channel_id=1, source_target_pairs={{0,1},{1,0},{2,3},{3,2},{4,5},{5,4},{6,7},{7,6},{8,9},{9,8},{10,11... | collective-permute-start | bytes 294920 | tf_op jit(solution)/shard_map/ppermute | solution.py:502
  40.1 18.7 %all-to-all-start.1 = ((bf16[64,8,768]{2,1,0:T(8,128)(2,1)}), bf16[64,8,768]{2,1,0:T(8,128)(2,1)S(1)}, u32[]{:S(2)}, u32[]{:S(2)}) async-start(bf16[64,8,768]{2,1,0:T(8,128)(2,1)} %bitcast.23), calls=%async_computation.1 | async-start | bytes 1572864 | tf_op jit(solution)/shard_map/all_to_all | solution.py:509
  59.4 4.0 %collective-permute-start.1 = (bf16[24,1024]{1,0:T(8,128)(2,1)S(1)}, bf16[24,1024]{1,0:T(8,128)(2,1)S(1)}, u32[]{:S(2)}, u32[]{:S(2)}) collective-permute-start(bf16[24,1024]{1,0:T(8,128)(2,1)S(1)} %get-tuple-element.24), channel_id=1, source_target_pairs={{0,1},{1,0},{2,3},{3,2},{4,5},{5,4},{6,7},{7,6},{8,9},{9,8},{10,11... | collective-permute-start | bytes 147464 | tf_op jit(solution)/shard_map/ppermute | solution.py:513

commit v4 on v3

--- a/solution.py
+++ b/solution.py
@@ -22,7 +22,8 @@
 TP = 32
 MiB = 1 << 20
 CORE_VMEM = 62
-GROUP = 4
+GROUPS = (5, 3)
+STARTS = tuple(sum(GROUPS[:n]) for n in range(len(GROUPS)))
 AHEAD = 2
 
 
@@ -58,8 +59,8 @@
         )
     ]
     stream = []
-    for first in range(0, HK, GROUP):
-        heads, rows = pl.ds(2 * first, 2 * GROUP), pl.ds(256 * first, 256 * GROUP)
+    for first, count in zip(STARTS, GROUPS):
+        heads, rows = pl.ds(2 * first, 2 * count), pl.ds(256 * first, 256 * count)
         sems = (stream_sem.at[len(stream)], stream_sem.at[len(stream) + 1])
         stream += [
             pltpu.make_async_copy(s_hbm.at[:, heads], state_ref.at[:, heads], sems[0]),
@@ -119,10 +120,10 @@
     gain = gain_in[...]
     outs = []
     written = []
-    for first in range(0, HK, GROUP):
-        group = range(first, first + GROUP)
-        span = slice(first * R, (first + GROUP) * R)
-        arrive(2 * first // GROUP)
+    for place, (first, count) in enumerate(zip(STARTS, GROUPS)):
+        group = range(first, first + count)
+        span = slice(first * R, (first + count) * R)
+        arrive(2 * place)
         for i in group:
             state = jnp.concatenate(
                 [state_ref[:, 2 * i + j].reshape(R * 128, 128).astype(BF16) for j in range(2)],
@@ -179,14 +180,14 @@
                 uu_ref[i, :, lanes] = jnp.concatenate([x[at] for x in late[j][:3]], axis=0)
                 f3_ref[i, :, lanes] = late[j][3][at]
         for source, target in ((ku_ref, k_hbm_out), (uu_ref, u_hbm_out), (f3_ref, f_hbm_out)):
-            span = pl.ds(first, GROUP)
+            span = pl.ds(first, count)
             written.append(
                 pltpu.make_async_copy(
                     source.at[span], target.at[span], out_sem.at[len(written)]
                 )
             )
             written[-1].start()
-        arrive(2 * first // GROUP + 1)
+        arrive(2 * place + 1)
         for i in group:
             part = dot(outs[i], w_in[i * 256 : (i + 1) * 256, :])
             if i == 0:
@@ -227,8 +228,8 @@
             pltpu.VMEM((2 * T, HK * R, 256), F32),
             pltpu.VMEM((TOK, D), F32),
             pltpu.SemaphoreType.DMA((10,)),
-            pltpu.SemaphoreType.DMA((2 * HK // GROUP,)),
-            pltpu.SemaphoreType.DMA((3 * HK // GROUP,)),
+            pltpu.SemaphoreType.DMA((2 * len(GROUPS),)),
+            pltpu.SemaphoreType.DMA((3 * len(GROUPS),)),
         ],
         compiler_params=pltpu.CompilerParams(vmem_limit_bytes=CORE_VMEM * MiB),
         cost_estimate=pl.CostEstimate(flops=10**9, bytes_accessed=17 * MiB, transcendentals=10**5),

time: 64.3 us -> 64.1 us (level)
  no operation moved by 1% of the time
where the time goes in v4:
time: 64.1 us; the launch traced here: 63.8 us
  blocking collectives  26.3 us (41%)
  Pallas kernels  18.9 us (29%)
  starting transfers between devices  9.31 us (15%)
  waiting for transfers between devices  7.94 us (12%)
  between operations  0.76 us (1%)
    all_to_all x1, blocking collectives, local(): arrived = lax.all_to_all(outbound.reshape(shape), 'ep', 0, 0, tiled=True)  26.3 us
    pallas_call x1, Pallas kernels, core_call(): pl.pallas_call(core_kernel, in_specs=[pl.BlockSpec(memory_space=pl.ANY)]...  7.31 us
    all_to_all x1, waiting for transfers between devices, local(): returned = lax.all_to_all(produced.reshape(shape), 'ep', 0, 0, tiled=True)  7.05 us
    pallas_call x1, Pallas kernels, state_call(): pl.pallas_call(state_kernel, in_specs=[pl.BlockSpec(memory_space=pl.ANY)]...  6.94 us
    all_to_all x1, starting transfers between devices, local(): returned = lax.all_to_all(produced.reshape(shape), 'ep', 0, 0, tiled=True)  4.65 us
    ppermute x1, starting transfers between devices, local(): got = lax.ppermute(give, 'hd', swap)  3.16 us
    pallas_call x1, Pallas kernels, expert_call(): pl.pallas_call(expert_kernel, out_specs=pl.BlockSpec(memory_space=pl.ANY)...  2.59 us
    ppermute x1, starting transfers between devices, local(): got = lax.ppermute(send, 'hd', swap)  1.5 us
  transfers between devices with their start and end apart: 3, of which 2 were waited for; matrix products, arithmetic and copies ran while one was open for 0% of the time, Pallas kernels for 12%

profile of v4, /device:TPU:1, one launch (start us, length us, event | category | flops | bytes accessed | tf_op | source)
XLA Modules:
  0.0 63.8 jit_solution(2636308467822439920)
XLA Ops:
  0.6 0.0 copy-start.3
  0.6 0.0 copy-start.4
  0.7 7.3 %core.1 = (f32[24,2048]{1,0:T(8,128)S(1)}, bf16[24,2048]{1,0:T(8,128)(2,1)S(1)}, f32[8,24,128]{2,1,0:T(8,128)}, f32[8,24,256]{2,1,0:T(8,128)}, f32[8,8,256]{2,1,0:T(8,128)}) custom-call(bf16[8,3,8,128]{3,2,1,0:T(8,128)(2,1)} %q_hbm.1, bf16[8,3,8,128]{3,2,1,0:T(8,128)(2,1)} %k_hbm.1, bf16[8,3,16,128]{3,2,1,0:T(8,128)(2,1)} %v_hbm.1, ...), custom_call_target="tpu_custom_call" | custom-call | flops 1000000000 | bytes 17825792 | tf_op jit(solution)/shard_map/core/pallas_call | solution.py:209
  8.0 0.0 copy-start.5
  8.0 0.0 copy-start
  8.0 0.0 copy-start.1
  8.0 0.0 copy-start.2
  8.0 1.5 %collective-permute-start = (bf16[24,2048]{1,0:T(8,128)(2,1)S(1)}, bf16[24,2048]{1,0:T(8,128)(2,1)S(1)}, u32[]{:S(2)}, u32[]{:S(2)}) collective-permute-start(bf16[24,2048]{1,0:T(8,128)(2,1)S(1)} %get-tuple-element.15), channel_id=1, source_target_pairs={{0,1},{1,0},{2,3},{3,2},{4,5},{5,4},{6,7},{7,6},{8,9},{9,8},{10,11... | collective-permute-start | bytes 294920 | tf_op jit(solution)/shard_map/ppermute | solution.py:503
  9.5 0.0 copy-done.3
  9.5 0.0 copy-done.4
  9.5 0.9 %tables.1 = (bf16[3,512,256]{2,1,0:T(8,128)(2,1)S(1)}, bf16[3,64,512]{2,1,0:T(8,128)(2,1)S(1)}) custom-call(s32[3,8,10]{2,1,0:T(8,128)S(1)} %bitcast.20, f32[3,8,10]{2,1,0:T(8,128)S(1)} %bitcast.21, f32[8,16,128,128]{3,2,1,0:T(8,128)} %s_hbm.3), custom_call_target="tpu_custom_call" | custom-call | flops 100000000 | bytes 1000000 | tf_op jit(solution)/shard_map/tables/pallas_call | solution.py:336
  10.5 0.0 collective-permute-done.got_ref
  10.5 0.0 copy-done.5
  10.5 0.5 dispatch.1
  11.0 26.3 %all_to_all.10 = bf16[64,8,768]{2,1,0:T(8,128)(2,1)S(1)} all-to-all(bf16[64,8,768]{2,1,0:T(8,128)(2,1)S(1)} %bitcast.19), channel_id=1, replica_groups=mesh['ep'=64,'hd'=2] {'ep'}, dimensions={0} | all-to-all | bytes 1572864 | tf_op jit(solution)/shard_map/all_to_all | solution.py:507
  37.2 0.0 copy-done
  37.3 2.6 %expert.1.after_ref = bf16[512,768]{1,0:T(8,128)(2,1)} custom-call(bf16[512,768]{1,0:T(8,128)(2,1)S(1)} %bitcast.18, bf16[1,2048,512]{2,1,0:T(8,128)(2,1)S(1)} %copy-done, bf16[1,2048,512]{2,1,0:T(8,128)(2,1)S(1)} %copy-done.1, bf16[1,512,2048]{2,1,0:T(8,128)(2,1)S(1)} %copy-done.2), custom_call_target="tpu_custom_call" | custom-call | flops 1200000000 | bytes 8000000 | tf_op jit(solution)/shard_map/expert/pallas_call | solution.py:407
  39.9 4.7 %all-to-all-start.1 = ((bf16[64,8,768]{2,1,0:T(8,128)(2,1)}), bf16[64,8,768]{2,1,0:T(8,128)(2,1)S(1)}, u32[]{:S(2)}, u32[]{:S(2)}) async-start(bf16[64,8,768]{2,1,0:T(8,128)(2,1)} %bitcast.23), calls=%async_computation.1 | async-start | bytes 1572864 | tf_op jit(solution)/shard_map/all_to_all | solution.py:510
  44.5 6.9 %state.1.state_ref = f32[8,16,128,128]{3,2,1,0:T(8,128)} custom-call(f32[8,16,128,128]{3,2,1,0:T(8,128)} %s_hbm.3, f32[8,24,128]{2,1,0:T(8,128)} %get-tuple-element.20.k_hbm, f32[8,24,256]{2,1,0:T(8,128)} %get-tuple-element.21.u_hbm, f32[8,8,256]{2,1,0:T(8,128)} %get-tuple-element.22.f_hbm, bf16[512,768]{1,0:T(8,128)(2,1)} %expert.1.after_ref), custom_call_target="tpu_custom_call" | custom-call | flops 1000000000 | bytes 17825792 | tf_op jit(solution)/shard_map/state/pallas_call | solution.py:286
  51.5 7.1 %all-to-all-done.1 = bf16[64,8,768]{2,1,0:T(8,128)(2,1)S(1)} async-done(((bf16[64,8,768]{2,1,0:T(8,128)(2,1)}), bf16[64,8,768]{2,1,0:T(8,128)(2,1)S(1)}, u32[]{:S(2)}, u32[]{:S(2)}) %all-to-all-start.1) | async-done | bytes 786464 | tf_op jit(solution)/shard_map/all_to_all | solution.py:510
  58.5 0.6 combine.1
  59.1 3.2 %collective-permute-start.1 = (bf16[24,1024]{1,0:T(8,128)(2,1)S(1)}, bf16[24,1024]{1,0:T(8,128)(2,1)S(1)}, u32[]{:S(2)}, u32[]{:S(2)}) collective-permute-start(bf16[24,1024]{1,0:T(8,128)(2,1)S(1)} %get-tuple-element.24), channel_id=1, source_target_pairs={{0,1},{1,0},{2,3},{3,2},{4,5},{5,4},{6,7},{7,6},{8,9},{9,8},{10,11... | collective-permute-start | bytes 147464 | tf_op jit(solution)/shard_map/ppermute | solution.py:514
  62.3 0.9 %collective-permute-done.1 = bf16[24,1024]{1,0:T(8,128)(2,1)S(1)} collective-permute-done((bf16[24,1024]{1,0:T(8,128)(2,1)S(1)}, bf16[24,1024]{1,0:T(8,128)(2,1)S(1)}, u32[]{:S(2)}, u32[]{:S(2)}) %collective-permute-start.1) | collective-permute-done | bytes 49184 | tf_op jit(solution)/shard_map/ppermute | solution.py:514
  63.2 0.6 fusion
  (2 shorter events, 0.0 us)
Async XLA Ops:
  0.6 8.9 %copy-start.3 = (s32[8,3,10]{2,0,1:T(8,128)S(1)}, s32[8,3,10]{2,0,1:T(8,128)}, u32[]{:S(2)}) copy-start(s32[8,3,10]{2,0,1:T(8,128)} %param.30) | copy-start | bytes 2884
  0.6 8.9 %copy-start.4 = (f32[8,3,10]{2,0,1:T(8,128)S(1)}, f32[8,3,10]{2,0,1:T(8,128)}, u32[]{:S(2)}) copy-start(f32[8,3,10]{2,0,1:T(8,128)} %param.31) | copy-start | bytes 2884
  8.0 2.5 %copy-start.5 = (f32[2048]{0:T(1024)S(1)}, f32[2048]{0:T(1024)}, u32[]{:S(2)}) copy-start(f32[2048]{0:T(1024)} %param.29) | copy-start | bytes 24580
  8.0 29.3 %copy-start = (bf16[1,2048,512]{2,1,0:T(8,128)(2,1)S(1)}, bf16[1,2048,512]{2,1,0:T(8,128)(2,1)}, u32[]{:S(2)}) copy-start(bf16[1,2048,512]{2,1,0:T(8,128)(2,1)} %gate_ref.1) | copy-start | bytes 6291460
  8.0 29.3 %copy-start.1 = (bf16[1,2048,512]{2,1,0:T(8,128)(2,1)S(1)}, bf16[1,2048,512]{2,1,0:T(8,128)(2,1)}, u32[]{:S(2)}) copy-start(bf16[1,2048,512]{2,1,0:T(8,128)(2,1)} %up_ref.1) | copy-start | bytes 6291460
  8.0 29.2 %copy-start.2 = (bf16[1,512,2048]{2,1,0:T(8,128)(2,1)S(1)}, bf16[1,512,2048]{2,1,0:T(8,128)(2,1)}, u32[]{:S(2)}) copy-start(bf16[1,512,2048]{2,1,0:T(8,128)(2,1)} %down_ref.1) | copy-start | bytes 6291460
  8.0 2.5 %collective-permute-start = (bf16[24,2048]{1,0:T(8,128)(2,1)S(1)}, bf16[24,2048]{1,0:T(8,128)(2,1)S(1)}, u32[]{:S(2)}, u32[]{:S(2)}) collective-permute-start(bf16[24,2048]{1,0:T(8,128)(2,1)S(1)} %get-tuple-element.15), channel_id=1, source_target_pairs={{0,1},{1,0},{2,3},{3,2},{4,5},{5,4},{6,7},{7,6},{8,9},{9,8},{10,11... | collective-permute-start | bytes 294920 | tf_op jit(solution)/shard_map/ppermute | solution.py:503
  39.9 18.7 %all-to-all-start.1 = ((bf16[64,8,768]{2,1,0:T(8,128)(2,1)}), bf16[64,8,768]{2,1,0:T(8,128)(2,1)S(1)}, u32[]{:S(2)}, u32[]{:S(2)}) async-start(bf16[64,8,768]{2,1,0:T(8,128)(2,1)} %bitcast.23), calls=%async_computation.1 | async-start | bytes 1572864 | tf_op jit(solution)/shard_map/all_to_all | solution.py:510
  59.1 4.0 %collective-permute-start.1 = (bf16[24,1024]{1,0:T(8,128)(2,1)S(1)}, bf16[24,1024]{1,0:T(8,128)(2,1)S(1)}, u32[]{:S(2)}, u32[]{:S(2)}) collective-permute-start(bf16[24,1024]{1,0:T(8,128)(2,1)S(1)} %get-tuple-element.24), channel_id=1, source_target_pairs={{0,1},{1,0},{2,3},{3,2},{4,5},{5,4},{6,7},{7,6},{8,9},{9,8},{10,11... | collective-permute-start | bytes 147464 | tf_op jit(solution)/shard_map/ppermute | solution.py:514

commit v5 on v4

--- a/solution.py
+++ b/solution.py
@@ -24,6 +24,7 @@
 CORE_VMEM = 62
 GROUPS = (5, 3)
 STARTS = tuple(sum(GROUPS[:n]) for n in range(len(GROUPS)))
+OUT_PIECES = 8
 AHEAD = 2
 
 
@@ -393,12 +394,14 @@
             at, side = c // 2 * CHIPS, c % 2 * 128
             wide[c, pl.ds(p, CHIPS, stride=PARTS), :] = y[at : at + CHIPS, side : side + 128]
     copies = []
-    for c in range(chunks):
-        lanes = slice(c * 128, (c + 1) * 128)
-        y_out[:, lanes] = wide[c].astype(BF16)
-        lanes = pl.ds(c * 128, 128)
-        copies.append(pltpu.make_async_copy(y_out.at[:, lanes], y_hbm.at[:, lanes], sem.at[c]))
-        copies[c].start()
+    rows_out = x_ref.shape[0] // OUT_PIECES
+    for n in range(OUT_PIECES):
+        rows = slice(n * rows_out, (n + 1) * rows_out)
+        for c in range(chunks):
+            y_out[rows, c * 128 : (c + 1) * 128] = wide[c, rows].astype(BF16)
+        rows = pl.ds(n * rows_out, rows_out)
+        copies.append(pltpu.make_async_copy(y_out.at[rows], y_hbm.at[rows], sem.at[n]))
+        copies[n].start()
     for copy in copies:
         copy.wait()
 
@@ -411,7 +414,7 @@
         scratch_shapes=[
             pltpu.VMEM((x.shape[1] // 128, x.shape[0], 128), F32),
             pltpu.VMEM(x.shape, BF16),
-            pltpu.SemaphoreType.DMA((x.shape[1] // 128,)),
+            pltpu.SemaphoreType.DMA((OUT_PIECES,)),
         ],
         compiler_params=pltpu.CompilerParams(vmem_limit_bytes=24 * MiB),
         cost_estimate=pl.CostEstimate(

time: 64.1 us -> 64.1 us (level)
  no operation moved by 1% of the time
where the time goes in v5:
time: 64.1 us; the launch traced here: 63.9 us
  blocking collectives  26.3 us (41%)
  Pallas kernels  19 us (30%)
  starting transfers between devices  9.31 us (15%)
  waiting for transfers between devices  7.94 us (12%)
  between operations  0.76 us (1%)
    all_to_all x1, blocking collectives, local(): arrived = lax.all_to_all(outbound.reshape(shape), 'ep', 0, 0, tiled=True)  26.3 us
    pallas_call x1, Pallas kernels, core_call(): pl.pallas_call(core_kernel, in_specs=[pl.BlockSpec(memory_space=pl.ANY)]...  7.31 us
    all_to_all x1, waiting for transfers between devices, local(): returned = lax.all_to_all(produced.reshape(shape), 'ep', 0, 0, tiled=True)  7.05 us
    pallas_call x1, Pallas kernels, state_call(): pl.pallas_call(state_kernel, in_specs=[pl.BlockSpec(memory_space=pl.ANY)]...  6.95 us
    all_to_all x1, starting transfers between devices, local(): returned = lax.all_to_all(produced.reshape(shape), 'ep', 0, 0, tiled=True)  4.65 us
    ppermute x1, starting transfers between devices, local(): got = lax.ppermute(give, 'hd', swap)  3.16 us
    pallas_call x1, Pallas kernels, expert_call(): pl.pallas_call(expert_kernel, out_specs=pl.BlockSpec(memory_space=pl.ANY)...  2.67 us
    ppermute x1, starting transfers between devices, local(): got = lax.ppermute(send, 'hd', swap)  1.5 us
  transfers between devices with their start and end apart: 3, of which 2 were waited for; matrix products, arithmetic and copies ran while one was open for 0% of the time, Pallas kernels for 12%

profile of v5, /device:TPU:1, one launch (start us, length us, event | category | flops | bytes accessed | tf_op | source)
XLA Modules:
  0.0 63.9 jit_solution(11884943393100983281)
XLA Ops:
  0.6 0.0 copy-start.3
  0.6 0.0 copy-start.4
  0.7 7.3 %core.1 = (f32[24,2048]{1,0:T(8,128)S(1)}, bf16[24,2048]{1,0:T(8,128)(2,1)S(1)}, f32[8,24,128]{2,1,0:T(8,128)}, f32[8,24,256]{2,1,0:T(8,128)}, f32[8,8,256]{2,1,0:T(8,128)}) custom-call(bf16[8,3,8,128]{3,2,1,0:T(8,128)(2,1)} %q_hbm.1, bf16[8,3,8,128]{3,2,1,0:T(8,128)(2,1)} %k_hbm.1, bf16[8,3,16,128]{3,2,1,0:T(8,128)(2,1)} %v_hbm.1, ...), custom_call_target="tpu_custom_call" | custom-call | flops 1000000000 | bytes 17825792 | tf_op jit(solution)/shard_map/core/pallas_call | solution.py:210
  8.0 0.0 copy-start.5
  8.0 0.0 copy-start
  8.0 0.0 copy-start.1
  8.0 0.0 copy-start.2
  8.0 1.5 %collective-permute-start = (bf16[24,2048]{1,0:T(8,128)(2,1)S(1)}, bf16[24,2048]{1,0:T(8,128)(2,1)S(1)}, u32[]{:S(2)}, u32[]{:S(2)}) collective-permute-start(bf16[24,2048]{1,0:T(8,128)(2,1)S(1)} %get-tuple-element.15), channel_id=1, source_target_pairs={{0,1},{1,0},{2,3},{3,2},{4,5},{5,4},{6,7},{7,6},{8,9},{9,8},{10,11... | collective-permute-start | bytes 294920 | tf_op jit(solution)/shard_map/ppermute | solution.py:506
  9.5 0.0 copy-done.3
  9.5 0.0 copy-done.4
  9.5 0.9 %tables.1 = (bf16[3,512,256]{2,1,0:T(8,128)(2,1)S(1)}, bf16[3,64,512]{2,1,0:T(8,128)(2,1)S(1)}) custom-call(s32[3,8,10]{2,1,0:T(8,128)S(1)} %bitcast.20, f32[3,8,10]{2,1,0:T(8,128)S(1)} %bitcast.21, f32[8,16,128,128]{3,2,1,0:T(8,128)} %s_hbm.3), custom_call_target="tpu_custom_call" | custom-call | flops 100000000 | bytes 1000000 | tf_op jit(solution)/shard_map/tables/pallas_call | solution.py:337
  10.5 0.0 collective-permute-done.got_ref
  10.5 0.0 copy-done.5
  10.5 0.5 dispatch.1
  11.0 26.3 %all_to_all.10 = bf16[64,8,768]{2,1,0:T(8,128)(2,1)S(1)} all-to-all(bf16[64,8,768]{2,1,0:T(8,128)(2,1)S(1)} %bitcast.19), channel_id=1, replica_groups=mesh['ep'=64,'hd'=2] {'ep'}, dimensions={0} | all-to-all | bytes 1572864 | tf_op jit(solution)/shard_map/all_to_all | solution.py:510
  37.2 0.0 copy-done
  37.3 2.7 %expert.1.after_ref = bf16[512,768]{1,0:T(8,128)(2,1)} custom-call(bf16[512,768]{1,0:T(8,128)(2,1)S(1)} %bitcast.18, bf16[1,2048,512]{2,1,0:T(8,128)(2,1)S(1)} %copy-done, bf16[1,2048,512]{2,1,0:T(8,128)(2,1)S(1)} %copy-done.1, bf16[1,512,2048]{2,1,0:T(8,128)(2,1)S(1)} %copy-done.2), custom_call_target="tpu_custom_call" | custom-call | flops 1200000000 | bytes 8000000 | tf_op jit(solution)/shard_map/expert/pallas_call | solution.py:410
  39.9 4.7 %all-to-all-start.1 = ((bf16[64,8,768]{2,1,0:T(8,128)(2,1)}), bf16[64,8,768]{2,1,0:T(8,128)(2,1)S(1)}, u32[]{:S(2)}, u32[]{:S(2)}) async-start(bf16[64,8,768]{2,1,0:T(8,128)(2,1)} %bitcast.23), calls=%async_computation.1 | async-start | bytes 1572864 | tf_op jit(solution)/shard_map/all_to_all | solution.py:513
  44.6 6.9 %state.1.state_ref = f32[8,16,128,128]{3,2,1,0:T(8,128)} custom-call(f32[8,16,128,128]{3,2,1,0:T(8,128)} %s_hbm.3, f32[8,24,128]{2,1,0:T(8,128)} %get-tuple-element.20.k_hbm, f32[8,24,256]{2,1,0:T(8,128)} %get-tuple-element.21.u_hbm, f32[8,8,256]{2,1,0:T(8,128)} %get-tuple-element.22.f_hbm, bf16[512,768]{1,0:T(8,128)(2,1)} %expert.1.after_ref), custom_call_target="tpu_custom_call" | custom-call | flops 1000000000 | bytes 17825792 | tf_op jit(solution)/shard_map/state/pallas_call | solution.py:287
  51.6 7.1 %all-to-all-done.1 = bf16[64,8,768]{2,1,0:T(8,128)(2,1)S(1)} async-done(((bf16[64,8,768]{2,1,0:T(8,128)(2,1)}), bf16[64,8,768]{2,1,0:T(8,128)(2,1)S(1)}, u32[]{:S(2)}, u32[]{:S(2)}) %all-to-all-start.1) | async-done | bytes 786464 | tf_op jit(solution)/shard_map/all_to_all | solution.py:513
  58.6 0.6 combine.1
  59.2 3.2 %collective-permute-start.1 = (bf16[24,1024]{1,0:T(8,128)(2,1)S(1)}, bf16[24,1024]{1,0:T(8,128)(2,1)S(1)}, u32[]{:S(2)}, u32[]{:S(2)}) collective-permute-start(bf16[24,1024]{1,0:T(8,128)(2,1)S(1)} %get-tuple-element.24), channel_id=1, source_target_pairs={{0,1},{1,0},{2,3},{3,2},{4,5},{5,4},{6,7},{7,6},{8,9},{9,8},{10,11... | collective-permute-start | bytes 147464 | tf_op jit(solution)/shard_map/ppermute | solution.py:517
  62.4 0.9 %collective-permute-done.1 = bf16[24,1024]{1,0:T(8,128)(2,1)S(1)} collective-permute-done((bf16[24,1024]{1,0:T(8,128)(2,1)S(1)}, bf16[24,1024]{1,0:T(8,128)(2,1)S(1)}, u32[]{:S(2)}, u32[]{:S(2)}) %collective-permute-start.1) | collective-permute-done | bytes 49184 | tf_op jit(solution)/shard_map/ppermute | solution.py:517
  63.3 0.6 fusion
  (2 shorter events, 0.0 us)
Async XLA Ops:
  0.6 8.9 %copy-start.3 = (s32[8,3,10]{2,0,1:T(8,128)S(1)}, s32[8,3,10]{2,0,1:T(8,128)}, u32[]{:S(2)}) copy-start(s32[8,3,10]{2,0,1:T(8,128)} %param.30) | copy-start | bytes 2884
  0.6 8.9 %copy-start.4 = (f32[8,3,10]{2,0,1:T(8,128)S(1)}, f32[8,3,10]{2,0,1:T(8,128)}, u32[]{:S(2)}) copy-start(f32[8,3,10]{2,0,1:T(8,128)} %param.31) | copy-start | bytes 2884
  8.0 2.5 %copy-start.5 = (f32[2048]{0:T(1024)S(1)}, f32[2048]{0:T(1024)}, u32[]{:S(2)}) copy-start(f32[2048]{0:T(1024)} %param.29) | copy-start | bytes 24580
  8.0 29.3 %copy-start = (bf16[1,2048,512]{2,1,0:T(8,128)(2,1)S(1)}, bf16[1,2048,512]{2,1,0:T(8,128)(2,1)}, u32[]{:S(2)}) copy-start(bf16[1,2048,512]{2,1,0:T(8,128)(2,1)} %gate_ref.1) | copy-start | bytes 6291460
  8.0 29.3 %copy-start.1 = (bf16[1,2048,512]{2,1,0:T(8,128)(2,1)S(1)}, bf16[1,2048,512]{2,1,0:T(8,128)(2,1)}, u32[]{:S(2)}) copy-start(bf16[1,2048,512]{2,1,0:T(8,128)(2,1)} %up_ref.1) | copy-start | bytes 6291460
  8.0 29.2 %copy-start.2 = (bf16[1,512,2048]{2,1,0:T(8,128)(2,1)S(1)}, bf16[1,512,2048]{2,1,0:T(8,128)(2,1)}, u32[]{:S(2)}) copy-start(bf16[1,512,2048]{2,1,0:T(8,128)(2,1)} %down_ref.1) | copy-start | bytes 6291460
  8.0 2.5 %collective-permute-start = (bf16[24,2048]{1,0:T(8,128)(2,1)S(1)}, bf16[24,2048]{1,0:T(8,128)(2,1)S(1)}, u32[]{:S(2)}, u32[]{:S(2)}) collective-permute-start(bf16[24,2048]{1,0:T(8,128)(2,1)S(1)} %get-tuple-element.15), channel_id=1, source_target_pairs={{0,1},{1,0},{2,3},{3,2},{4,5},{5,4},{6,7},{7,6},{8,9},{9,8},{10,11... | collective-permute-start | bytes 294920 | tf_op jit(solution)/shard_map/ppermute | solution.py:506
  39.9 18.7 %all-to-all-start.1 = ((bf16[64,8,768]{2,1,0:T(8,128)(2,1)}), bf16[64,8,768]{2,1,0:T(8,128)(2,1)S(1)}, u32[]{:S(2)}, u32[]{:S(2)}) async-start(bf16[64,8,768]{2,1,0:T(8,128)(2,1)} %bitcast.23), calls=%async_computation.1 | async-start | bytes 1572864 | tf_op jit(solution)/shard_map/all_to_all | solution.py:513
  59.2 4.0 %collective-permute-start.1 = (bf16[24,1024]{1,0:T(8,128)(2,1)S(1)}, bf16[24,1024]{1,0:T(8,128)(2,1)S(1)}, u32[]{:S(2)}, u32[]{:S(2)}) collective-permute-start(bf16[24,1024]{1,0:T(8,128)(2,1)S(1)} %get-tuple-element.24), channel_id=1, source_target_pairs={{0,1},{1,0},{2,3},{3,2},{4,5},{5,4},{6,7},{7,6},{8,9},{9,8},{10,11... | collective-permute-start | bytes 147464 | tf_op jit(solution)/shard_map/ppermute | solution.py:517
